TPU v7x, 32 devices: a whole 2x2x4 slice. The times are simulated.
32 devices in a mesh: sec: 4 (over y, x), blk: 8 (over z, core).
Axes of the slice: x: 2, y: 2, z: 4, core: 2. Of those that a mesh axis runs over, the one named last changes fastest.
Arguments:
- tiles: bfloat16 [4, 8, 1024, 1024], P('sec', 'blk'), may hold values from -6 to 6
- row_taps: bfloat16 [4, 8, 9, 4, 512], P('sec', 'blk'), may hold values from -0.25 to 1
- col_taps: bfloat16 [4, 8, 9, 4, 512], P('sec', 'blk'), may hold values from -0.25 to 1
- row_starts: int32 [4, 8, 9, 512], P('sec', 'blk'), may hold values from 0 to 636, as said below
- col_starts: int32 [4, 8, 9, 512], P('sec', 'blk'), may hold values from 0 to 636, as said below
- feather_rows: bfloat16 [4, 8, 512], P('sec', 'blk'), may hold values from 0.19921875 to 1
- feather_cols: bfloat16 [4, 8, 512], P('sec', 'blk'), may hold values from 0.19921875 to 1
- footprint: int32 [4, 8, 9], P('sec', 'blk'), may hold values from 0 to 1, as said below
- offsets: int32 [4, 8, 9, 2], P('sec', 'blk'), may hold values from 0 to 384
Outputs:
- blended: bfloat16 [4, 8, 512, 512], P('sec', 'blk')
- level: bfloat16 [4, 8, 256, 256], P('sec', 'blk')
Inputs may be any that keep to these rules, and one draw needn't show every extreme that they name: `footprint`: the centre slot (k = 4) is 1 for every block; a slot whose tile lies outside the grid of 2 by 4 positions is 0; the other slots are 0 or 1 independently. `row_starts`: output row 0 starts at 0 and output row 511 at 636; starts never exceed 640 - 4. `col_starts`: output column 0 starts at 0 and output column 511 at 636; starts never exceed 640 - 4.
All inputs are finite; a program needn't handle non-finite values.
Results may differ from a plain program's by a relative error of at most 0.0085.
Values may be sent and summed in bfloat16 or wider, within the bound.
No kernel may reach another device: no remote copies, remote signals or barrier semaphores. Data moves between devices by JAX's collectives and lax.ppermute only.
A program may use at most 128 MiB of HBM per device.

v0:
```python
import jax
import jax.numpy as jnp
from jax import lax
from jax.sharding import PartitionSpec as P

BAND = 640
GY = 4


SLOT_PAIRS = [(-1, -1), (-1, 0), (-1, 1), (0, -1), (0, 0), (0, 1), (1, -1), (1, 0), (1, 1)]


def from_behind(value, axis, by):
    devices = lax.axis_size(axis)
    pairs = [(i, i + by) for i in range(devices) if 0 <= i + by < devices]
    return lax.ppermute(value, axis, pairs)


def padded(cells, sides, width):
    for axis, dim in sides:
        count = lax.axis_size(axis)
        ends = count - 1
        head = lax.slice_in_dim(cells, 0, width, axis=dim)
        tail = lax.slice_in_dim(cells, cells.shape[dim] - width, cells.shape[dim], axis=dim)
        cells = jnp.concatenate(
            [
                lax.ppermute(tail, axis, [(i, (i + 1) % count) for i in range(ends)]),
                cells,
                lax.ppermute(head, axis, [((i + 1) % count, i) for i in range(ends)]),
            ],
            axis=dim,
        )
    return cells


def apply_taps(tile, corner, row_first, row_weight, col_first, col_weight, band):
    window = lax.dynamic_slice(tile, (corner[0], corner[1]), (band, band))
    rows = jnp.zeros((row_first.shape[0], band), jnp.float32)
    for tap in range(row_weight.shape[0]):
        picked = jnp.take(window, row_first + tap, axis=0).astype(jnp.float32)
        rows = rows + row_weight[tap].astype(jnp.float32)[:, None] * picked
    flipped = rows.astype(jnp.bfloat16).T
    contrib_t = jnp.zeros((col_first.shape[0], row_first.shape[0]), jnp.float32)
    for tap in range(col_weight.shape[0]):
        picked = jnp.take(flipped, col_first + tap, axis=0).astype(jnp.float32)
        contrib_t = contrib_t + col_weight[tap].astype(jnp.float32)[:, None] * picked
    return contrib_t.T.astype(jnp.bfloat16)


def box_mean(field):
    total = (
        field[..., 0::2, 0::2]
        + field[..., 1::2, 0::2]
        + field[..., 0::2, 1::2]
        + field[..., 1::2, 1::2]
    )
    return total * 0.25


def partial_band(band):

    def apply_band(tile, corner, row_first, row_weight, col_first, col_weight):
        return apply_taps(tile, corner, row_first, row_weight, col_first, col_weight, band)

    return apply_band


def per_device(
    tiles,
    row_taps,
    col_taps,
    row_starts,
    col_starts,
    feather_rows,
    feather_cols,
    footprint,
    offsets,
):
    sections = tiles.shape[0]
    edge = row_starts.shape[3]
    batched = jax.vmap(partial_band(BAND))
    numer = jnp.zeros((sections, edge, edge), jnp.float32)
    denom = jnp.zeros((sections, edge, edge), jnp.float32)
    for slot_index, pair in enumerate(SLOT_PAIRS):
        row_step, col_step = pair
        offset_by = -(col_step * GY + row_step)
        if offset_by == 0:
            contrib = batched(
                tiles[:, 0],
                offsets[:, 0, slot_index],
                row_starts[:, 0, slot_index],
                row_taps[:, 0, slot_index],
                col_starts[:, 0, slot_index],
                col_taps[:, 0, slot_index],
            )
            prof_rows = feather_rows[:, 0]
            prof_cols = feather_cols[:, 0]
        else:
            moved = from_behind((tiles, feather_rows, feather_cols), "blk", offset_by)
            contrib = batched(
                moved[0][:, 0],
                offsets[:, 0, slot_index],
                row_starts[:, 0, slot_index],
                row_taps[:, 0, slot_index],
                col_starts[:, 0, slot_index],
                col_taps[:, 0, slot_index],
            )
            prof_rows = moved[1][:, 0]
            prof_cols = moved[2][:, 0]
        used = footprint[:, 0, slot_index].astype(jnp.float32)
        weight = (
            used[:, None, None]
            * prof_rows.astype(jnp.float32)[:, :, None]
            * prof_cols.astype(jnp.float32)[:, None, :]
        )
        numer = numer + weight * contrib.astype(jnp.float32)
        denom = denom + weight
    blended = (numer / denom).astype(jnp.bfloat16)[:, None]
    total_sections = sections * lax.axis_size("sec")
    global_index = lax.axis_index("sec") * sections + jnp.arange(sections)
    present = (
        4.0
        - (global_index == 0).astype(jnp.float32)
        - (global_index == total_sections - 1).astype(jnp.float32)
    )
    extended = padded(blended, (("sec", 0),), 1).astype(jnp.float32)
    zsum = extended[:-2] + 2.0 * extended[1:-1] + extended[2:]
    level = box_mean(zsum / present[:, None, None, None])
    return (blended, level.astype(jnp.bfloat16))


def solution(mesh):
    return jax.shard_map(
        per_device,
        mesh=mesh,
        in_specs=(
            P("sec", "blk", None, None),
            P("sec", "blk", None, None, None),
            P("sec", "blk", None, None, None),
            P("sec", "blk", None, None),
            P("sec", "blk", None, None),
            P("sec", "blk", None),
            P("sec", "blk", None),
            P("sec", "blk", None),
            P("sec", "blk", None, None),
        ),
        out_specs=(P("sec", "blk", None, None), P("sec", "blk", None, None)),
        check_vma=False,
    )
```

profile of v0, /device:TPU:1, one launch (start us, length us, event | category | flops | bytes accessed | tf_op | source)
XLA Modules:
  0.0 707.4 jit_solution(16352370178070747203)
XLA Ops:
  0.6 6.3 collective-permute-start.11
  8.3 8.4 %collective-permute-start = (bf16[1,1,512]{2,1,0:T(2,128)(2,1)}, bf16[1,1,512]{2,1,0:T(2,128)(2,1)S(1)}, u32[]{:S(2)}, u32[]{:S(2)}) collective-permute-start(bf16[1,1,512]{2,1,0:T(2,128)(2,1)} %param.18), channel_id=1, source_target_pairs={{0,5},{1,6},{2,7},{8,13},{9,14},{10,15},{16,21},{17,22},{18,23},{2... | collective-permute-start | bytes 3080 | tf_op jit(solution)/shard_map/ppermute | solution.py:16
  68.8 6.0 gather_fusion.35
  97.6 5.8 gather_fusion.38
  126.6 7.5 %collective-permute-start.15 = (bf16[1,1,512]{2,1,0:T(2,128)(2,1)S(1)}, bf16[1,1,512]{2,1,0:T(2,128)(2,1)S(1)}, u32[]{:S(2)}, u32[]{:S(2)}) collective-permute-start(bf16[1,1,512]{2,1,0:T(2,128)(2,1)S(1)} %copy-done.55), channel_id=1, source_target_pairs={{0,3},{1,4},{2,5},{3,6},{4,7},{8,11},{9,12},{10,13},{11,14},{12,15... | collective-permute-start | bytes 3080 | tf_op jit(solution)/shard_map/ppermute | solution.py:16
  151.1 38.8 %collective-permute-done.1 = bf16[1,1,512]{2,1,0:T(2,128)(2,1)S(1)} collective-permute-done((bf16[1,1,512]{2,1,0:T(2,128)(2,1)S(1)}, bf16[1,1,512]{2,1,0:T(2,128)(2,1)S(1)}, u32[]{:S(2)}, u32[]{:S(2)}) %collective-permute-start.1) | collective-permute-done | bytes 1056 | tf_op jit(solution)/shard_map/ppermute | solution.py:16
  196.9 25.4 %collective-permute-start.5 = (bf16[1,1,1024,1024]{3,2,1,0:T(8,128)(2,1)}, bf16[1,1,1024,1024]{3,2,1,0:T(8,128)(2,1)}, u32[]{:S(2)}, u32[]{:S(2)}) collective-permute-start(bf16[1,1,1024,1024]{3,2,1,0:T(8,128)(2,1)} %param.13), channel_id=1, source_target_pairs={{0,1},{1,2},{2,3},{3,4},{4,5},{5,6},{6,7},{8,9},{9,10},{10,11},{11... | collective-permute-start | bytes 6291464 | tf_op jit(solution)/shard_map/ppermute | solution.py:16
  231.5 14.0 %collective-permute-done.4 = bf16[1,1,512]{2,1,0:T(2,128)(2,1)S(1)} collective-permute-done((bf16[1,1,512]{2,1,0:T(2,128)(2,1)S(1)}, bf16[1,1,512]{2,1,0:T(2,128)(2,1)S(1)}, u32[]{:S(2)}, u32[]{:S(2)}) %collective-permute-start.4) | collective-permute-done | bytes 1056 | tf_op jit(solution)/shard_map/ppermute | solution.py:16
  271.3 6.0 gather_fusion.27
  316.4 6.0 gather_fusion.43
  324.6 5.8 gather_fusion.44
  330.4 5.8 gather_fusion.45
  336.2 5.8 gather_fusion.46
  347.8 12.9 %collective-permute-start.2 = (bf16[1,1,1024,1024]{3,2,1,0:T(8,128)(2,1)}, bf16[1,1,1024,1024]{3,2,1,0:T(8,128)(2,1)}, u32[]{:S(2)}, u32[]{:S(2)}) collective-permute-start(bf16[1,1,1024,1024]{3,2,1,0:T(8,128)(2,1)} %param.13), channel_id=1, source_target_pairs={{0,5},{1,6},{2,7},{8,13},{9,14},{10,15},{16,21},{17,22},{18,23},{2... | collective-permute-start | bytes 6291464 | tf_op jit(solution)/shard_map/ppermute | solution.py:16
  373.1 6.0 gather_fusion.51
  381.4 5.8 gather_fusion.52
  393.0 5.8 gather_fusion.54
  416.9 6.0 gather_fusion.11
  430.9 6.0 gather_fusion.13
  460.8 6.0 gather_fusion.19
  510.5 5.8 gather_fusion.60
  516.4 5.8 gather_fusion.61
  562.7 5.8 gather_fusion.70
  568.5 6.0 gather_fusion.71
  591.7 5.8 gather_fusion.4
  615.7 16.6 %fusion.21 = bf16[1,1,512,512]{2,3,1,0:T(8,128)(2,1)S(1)} fusion(bf16[512,512]{1,0:T(8,128)(2,1)} %gather_fusion.71, pred[512]{0:T(512)(128)(4,1)} %get-tuple-element.364, f32[512]{0:T(512)S(1)} %bitcast.1341, bf16[512,512]{1,0:T(8,128)(2,1)} %gather_fusion.70, pred[512]{0:T(512)(128)(4,1)} %get-tuple-element.362, f32[512]{0:T(512)S(1)} %bitcast.1342, ...), kind=kLoop, calls=%fused_computation.212 | loop fusion | flops 49545216 | bytes 19527680 | tf_op jit(solution)/shard_map/broadcast_in_dim | solution.py:118
  637.7 7.1 %collective-permute-done.24 = bf16[1,1,512,512]{2,3,1,0:T(8,128)(2,1)S(1)} collective-permute-done((bf16[1,1,512,512]{2,3,1,0:T(8,128)(2,1)S(1)}, bf16[1,1,512,512]{2,3,1,0:T(8,128)(2,1)S(1)}, u32[]{:S(2)}, u32[]{:S(2)}) %collective-permute-start.24) | collective-permute-done | bytes 524320 | tf_op jit(solution)/shard_map/ppermute | solution.py:27
  644.8 12.9 %collective-permute-done.25 = bf16[1,1,512,512]{2,3,1,0:T(8,128)(2,1)S(1)} collective-permute-done((bf16[1,1,512,512]{2,3,1,0:T(8,128)(2,1)S(1)}, bf16[1,1,512,512]{2,3,1,0:T(8,128)(2,1)S(1)}, u32[]{:S(2)}, u32[]{:S(2)}) %collective-permute-start.25) | collective-permute-done | bytes 524320 | tf_op jit(solution)/shard_map/ppermute | solution.py:29
  658.3 12.0 %slice.600 = f32[1,1,256,256]{2,3,1,0:T(8,128)S(1)} slice(f32[1,1,512,512]{2,3,1,0:T(8,128)S(1)} %fusion.9), slice={[0:1:1], [0:1:1], [0:512:2], [0:512:2]} | slice | bytes 524288 | tf_op jit(solution)/shard_map/slice | solution.py:52
  670.4 11.8 %slice.601 = f32[1,1,256,256]{2,3,1,0:T(8,128)S(1)} slice(f32[1,1,512,512]{2,3,1,0:T(8,128)S(1)} %fusion.9), slice={[0:1:1], [0:1:1], [1:512:2], [0:512:2]} | slice | bytes 524288 | tf_op jit(solution)/shard_map/slice | solution.py:53
  682.2 11.8 %slice.602 = f32[1,1,256,256]{2,3,1,0:T(8,128)S(1)} slice(f32[1,1,512,512]{2,3,1,0:T(8,128)S(1)} %fusion.9), slice={[0:1:1], [0:1:1], [0:512:2], [1:512:2]} | slice | bytes 524288 | tf_op jit(solution)/shard_map/slice | solution.py:54
  694.0 12.1 %slice.603 = f32[1,1,256,256]{2,3,1,0:T(8,128)S(1)} slice(f32[1,1,512,512]{2,3,1,0:T(8,128)S(1)} %fusion.9), slice={[0:1:1], [0:1:1], [1:512:2], [1:512:2]} | slice | bytes 524288 | tf_op jit(solution)/shard_map/slice | solution.py:55
  (410 shorter events, 361.2 us)
Async XLA Ops:
  0.6 256.4 %collective-permute-start.11 = (bf16[1,1,1024,1024]{3,2,1,0:T(8,128)(2,1)}, bf16[1,1,1024,1024]{3,2,1,0:T(8,128)(2,1)}, u32[]{:S(2)}, u32[]{:S(2)}) collective-permute-start(bf16[1,1,1024,1024]{3,2,1,0:T(8,128)(2,1)} %param.13), channel_id=1, source_target_pairs={{0,4},{1,5},{2,6},{3,7},{8,12},{9,13},{10,14},{11,15},{16,20},{17,... | collective-permute-start | bytes 6291464 | tf_op jit(solution)/shard_map/ppermute | solution.py:16
  7.0 295.8 %collective-permute-start.14 = (bf16[1,1,1024,1024]{3,2,1,0:T(8,128)(2,1)}, bf16[1,1,1024,1024]{3,2,1,0:T(8,128)(2,1)}, u32[]{:S(2)}, u32[]{:S(2)}) collective-permute-start(bf16[1,1,1024,1024]{3,2,1,0:T(8,128)(2,1)} %param.13), channel_id=1, source_target_pairs={{4,0},{5,1},{6,2},{7,3},{12,8},{13,9},{14,10},{15,11},{20,16},{21,... | collective-permute-start | bytes 6291464 | tf_op jit(solution)/shard_map/ppermute | solution.py:16
  8.3 117.0 %collective-permute-start = (bf16[1,1,512]{2,1,0:T(2,128)(2,1)}, bf16[1,1,512]{2,1,0:T(2,128)(2,1)S(1)}, u32[]{:S(2)}, u32[]{:S(2)}) collective-permute-start(bf16[1,1,512]{2,1,0:T(2,128)(2,1)} %param.18), channel_id=1, source_target_pairs={{0,5},{1,6},{2,7},{8,13},{9,14},{10,15},{16,21},{17,22},{18,23},{2... | collective-permute-start | bytes 3080 | tf_op jit(solution)/shard_map/ppermute | solution.py:16
  16.6 109.9 %collective-permute-start.6 = (bf16[1,1,512]{2,1,0:T(2,128)(2,1)}, bf16[1,1,512]{2,1,0:T(2,128)(2,1)S(1)}, u32[]{:S(2)}, u32[]{:S(2)}) collective-permute-start(bf16[1,1,512]{2,1,0:T(2,128)(2,1)} %param.18), channel_id=1, source_target_pairs={{3,0},{4,1},{5,2},{6,3},{7,4},{11,8},{12,9},{13,10},{14,11},{15,12... | collective-permute-start | bytes 3080 | tf_op jit(solution)/shard_map/ppermute | solution.py:16
  17.9 116.1 %collective-permute-start.9 = (bf16[1,1,512]{2,1,0:T(2,128)(2,1)}, bf16[1,1,512]{2,1,0:T(2,128)(2,1)S(1)}, u32[]{:S(2)}, u32[]{:S(2)}) collective-permute-start(bf16[1,1,512]{2,1,0:T(2,128)(2,1)} %param.18), channel_id=1, source_target_pairs={{0,4},{1,5},{2,6},{3,7},{8,12},{9,13},{10,14},{11,15},{16,20},{17,... | collective-permute-start | bytes 3080 | tf_op jit(solution)/shard_map/ppermute | solution.py:16
  68.8 6.9 copy-start.7
  68.8 7.6 %copy-start.6 = (s32[1,1,9]{2,1,0:T(1,128)S(1)}, s32[1,1,9]{2,1,0:T(1,128)}, u32[]{:S(2)}) copy-start(s32[1,1,9]{2,1,0:T(1,128)} %param.20) | copy-start | bytes 112
  68.8 8.9 %copy-start.55 = (bf16[1,1,512]{2,1,0:T(2,128)(2,1)S(1)}, bf16[1,1,512]{2,1,0:T(2,128)(2,1)}, u32[]{:S(2)}) copy-start(bf16[1,1,512]{2,1,0:T(2,128)(2,1)} %param.18) | copy-start | bytes 3076
  74.8 6.8 copy-start
  103.4 11.4 %copy-start.54 = (bf16[1,1,512]{2,1,0:T(2,128)(2,1)S(1)}, bf16[1,1,512]{2,1,0:T(2,128)(2,1)}, u32[]{:S(2)}) copy-start(bf16[1,1,512]{2,1,0:T(2,128)(2,1)} %param.19) | copy-start | bytes 3076
  125.2 11.3 %collective-permute-start.12 = (bf16[1,1,512]{2,1,0:T(2,128)(2,1)S(1)}, bf16[1,1,512]{2,1,0:T(2,128)(2,1)S(1)}, u32[]{:S(2)}, u32[]{:S(2)}) collective-permute-start(bf16[1,1,512]{2,1,0:T(2,128)(2,1)S(1)} %copy-done.55), channel_id=1, source_target_pairs={{4,0},{5,1},{6,2},{7,3},{12,8},{13,9},{14,10},{15,11},{20,16},{21,... | collective-permute-start | bytes 3080 | tf_op jit(solution)/shard_map/ppermute | solution.py:16
  126.6 11.3 %collective-permute-start.15 = (bf16[1,1,512]{2,1,0:T(2,128)(2,1)S(1)}, bf16[1,1,512]{2,1,0:T(2,128)(2,1)S(1)}, u32[]{:S(2)}, u32[]{:S(2)}) collective-permute-start(bf16[1,1,512]{2,1,0:T(2,128)(2,1)S(1)} %copy-done.55), channel_id=1, source_target_pairs={{0,3},{1,4},{2,5},{3,6},{4,7},{8,11},{9,12},{10,13},{11,14},{12,15... | collective-permute-start | bytes 3080 | tf_op jit(solution)/shard_map/ppermute | solution.py:16
  134.0 5.2 collective-permute-start.18
  136.6 8.6 %collective-permute-start.21 = (bf16[1,1,512]{2,1,0:T(2,128)(2,1)S(1)}, bf16[1,1,512]{2,1,0:T(2,128)(2,1)S(1)}, u32[]{:S(2)}, u32[]{:S(2)}) collective-permute-start(bf16[1,1,512]{2,1,0:T(2,128)(2,1)S(1)} %copy-done.55), channel_id=1, source_target_pairs={{5,0},{6,1},{7,2},{13,8},{14,9},{15,10},{21,16},{22,17},{23,18},{2... | collective-permute-start | bytes 3080 | tf_op jit(solution)/shard_map/ppermute | solution.py:16
  137.8 10.0 %collective-permute-start.7 = (bf16[1,1,512]{2,1,0:T(2,128)(2,1)S(1)}, bf16[1,1,512]{2,1,0:T(2,128)(2,1)S(1)}, u32[]{:S(2)}, u32[]{:S(2)}) collective-permute-start(bf16[1,1,512]{2,1,0:T(2,128)(2,1)S(1)} %copy-done.54), channel_id=1, source_target_pairs={{3,0},{4,1},{5,2},{6,3},{7,4},{11,8},{12,9},{13,10},{14,11},{15,12... | collective-permute-start | bytes 3080 | tf_op jit(solution)/shard_map/ppermute | solution.py:16
  139.2 9.9 %collective-permute-start.10 = (bf16[1,1,512]{2,1,0:T(2,128)(2,1)S(1)}, bf16[1,1,512]{2,1,0:T(2,128)(2,1)S(1)}, u32[]{:S(2)}, u32[]{:S(2)}) collective-permute-start(bf16[1,1,512]{2,1,0:T(2,128)(2,1)S(1)} %copy-done.54), channel_id=1, source_target_pairs={{0,4},{1,5},{2,6},{3,7},{8,12},{9,13},{10,14},{11,15},{16,20},{17,... | collective-permute-start | bytes 3080 | tf_op jit(solution)/shard_map/ppermute | solution.py:16
  145.2 202.6 %collective-permute-start.17 = (bf16[1,1,1024,1024]{3,2,1,0:T(8,128)(2,1)}, bf16[1,1,1024,1024]{3,2,1,0:T(8,128)(2,1)}, u32[]{:S(2)}, u32[]{:S(2)}) collective-permute-start(bf16[1,1,1024,1024]{3,2,1,0:T(8,128)(2,1)} %param.13), channel_id=1, source_target_pairs={{0,3},{1,4},{2,5},{3,6},{4,7},{8,11},{9,12},{10,13},{11,14},{12,15... | collective-permute-start | bytes 6291464 | tf_op jit(solution)/shard_map/ppermute | solution.py:16
  147.9 42.0 %collective-permute-start.1 = (bf16[1,1,512]{2,1,0:T(2,128)(2,1)S(1)}, bf16[1,1,512]{2,1,0:T(2,128)(2,1)S(1)}, u32[]{:S(2)}, u32[]{:S(2)}) collective-permute-start(bf16[1,1,512]{2,1,0:T(2,128)(2,1)S(1)} %copy-done.54), channel_id=1, source_target_pairs={{0,5},{1,6},{2,7},{8,13},{9,14},{10,15},{16,21},{17,22},{18,23},{2... | collective-permute-start | bytes 3080 | tf_op jit(solution)/shard_map/ppermute | solution.py:16
  149.2 42.0 %collective-permute-start.13 = (bf16[1,1,512]{2,1,0:T(2,128)(2,1)S(1)}, bf16[1,1,512]{2,1,0:T(2,128)(2,1)S(1)}, u32[]{:S(2)}, u32[]{:S(2)}) collective-permute-start(bf16[1,1,512]{2,1,0:T(2,128)(2,1)S(1)} %copy-done.54), channel_id=1, source_target_pairs={{4,0},{5,1},{6,2},{7,3},{12,8},{13,9},{14,10},{15,11},{20,16},{21,... | collective-permute-start | bytes 3080 | tf_op jit(solution)/shard_map/ppermute | solution.py:16
  189.9 7.0 collective-permute-start.16
  191.2 31.1 %collective-permute-start.19 = (bf16[1,1,512]{2,1,0:T(2,128)(2,1)S(1)}, bf16[1,1,512]{2,1,0:T(2,128)(2,1)S(1)}, u32[]{:S(2)}, u32[]{:S(2)}) collective-permute-start(bf16[1,1,512]{2,1,0:T(2,128)(2,1)S(1)} %copy-done.54), channel_id=1, source_target_pairs={{1,0},{2,1},{3,2},{4,3},{5,4},{6,5},{7,6},{9,8},{10,9},{11,10},{12... | collective-permute-start | bytes 3080 | tf_op jit(solution)/shard_map/ppermute | solution.py:16
  196.9 207.7 %collective-permute-start.5 = (bf16[1,1,1024,1024]{3,2,1,0:T(8,128)(2,1)}, bf16[1,1,1024,1024]{3,2,1,0:T(8,128)(2,1)}, u32[]{:S(2)}, u32[]{:S(2)}) collective-permute-start(bf16[1,1,1024,1024]{3,2,1,0:T(8,128)(2,1)} %param.13), channel_id=1, source_target_pairs={{0,1},{1,2},{2,3},{3,4},{4,5},{5,6},{6,7},{8,9},{9,10},{10,11},{11... | collective-permute-start | bytes 6291464 | tf_op jit(solution)/shard_map/ppermute | solution.py:16
  222.3 6.7 collective-permute-start.22
  229.0 16.6 %collective-permute-start.4 = (bf16[1,1,512]{2,1,0:T(2,128)(2,1)S(1)}, bf16[1,1,512]{2,1,0:T(2,128)(2,1)S(1)}, u32[]{:S(2)}, u32[]{:S(2)}) collective-permute-start(bf16[1,1,512]{2,1,0:T(2,128)(2,1)S(1)} %copy-done.54), channel_id=1, source_target_pairs={{0,1},{1,2},{2,3},{3,4},{4,5},{5,6},{6,7},{8,9},{9,10},{10,11},{11... | collective-permute-start | bytes 3080 | tf_op jit(solution)/shard_map/ppermute | solution.py:16
  245.6 9.7 %collective-permute-start.3 = (bf16[1,1,512]{2,1,0:T(2,128)(2,1)S(1)}, bf16[1,1,512]{2,1,0:T(2,128)(2,1)S(1)}, u32[]{:S(2)}, u32[]{:S(2)}) collective-permute-start(bf16[1,1,512]{2,1,0:T(2,128)(2,1)S(1)} %copy-done.55), channel_id=1, source_target_pairs={{0,1},{1,2},{2,3},{3,4},{4,5},{5,6},{6,7},{8,9},{9,10},{10,11},{11... | collective-permute-start | bytes 3080 | tf_op jit(solution)/shard_map/ppermute | solution.py:16
  255.2 193.3 %collective-permute-start.8 = (bf16[1,1,1024,1024]{3,2,1,0:T(8,128)(2,1)}, bf16[1,1,1024,1024]{3,2,1,0:T(8,128)(2,1)}, u32[]{:S(2)}, u32[]{:S(2)}) collective-permute-start(bf16[1,1,1024,1024]{3,2,1,0:T(8,128)(2,1)} %param.13), channel_id=1, source_target_pairs={{3,0},{4,1},{5,2},{6,3},{7,4},{11,8},{12,9},{13,10},{14,11},{15,12... | collective-permute-start | bytes 6291464 | tf_op jit(solution)/shard_map/ppermute | solution.py:16
  257.1 235.2 %collective-permute-start.20 = (bf16[1,1,1024,1024]{3,2,1,0:T(8,128)(2,1)}, bf16[1,1,1024,1024]{3,2,1,0:T(8,128)(2,1)}, u32[]{:S(2)}, u32[]{:S(2)}) collective-permute-start(bf16[1,1,1024,1024]{3,2,1,0:T(8,128)(2,1)} %param.13), channel_id=1, source_target_pairs={{1,0},{2,1},{3,2},{4,3},{5,4},{6,5},{7,6},{9,8},{10,9},{11,10},{12... | collective-permute-start | bytes 6291464 | tf_op jit(solution)/shard_map/ppermute | solution.py:16
  302.8 231.0 %collective-permute-start.23 = (bf16[1,1,1024,1024]{3,2,1,0:T(8,128)(2,1)}, bf16[1,1,1024,1024]{3,2,1,0:T(8,128)(2,1)}, u32[]{:S(2)}, u32[]{:S(2)}) collective-permute-start(bf16[1,1,1024,1024]{3,2,1,0:T(8,128)(2,1)} %param.13), channel_id=1, source_target_pairs={{5,0},{6,1},{7,2},{13,8},{14,9},{15,10},{21,16},{22,17},{23,18},{2... | collective-permute-start | bytes 6291464 | tf_op jit(solution)/shard_map/ppermute | solution.py:16
  347.8 226.7 %collective-permute-start.2 = (bf16[1,1,1024,1024]{3,2,1,0:T(8,128)(2,1)}, bf16[1,1,1024,1024]{3,2,1,0:T(8,128)(2,1)}, u32[]{:S(2)}, u32[]{:S(2)}) collective-permute-start(bf16[1,1,1024,1024]{3,2,1,0:T(8,128)(2,1)} %param.13), channel_id=1, source_target_pairs={{0,5},{1,6},{2,7},{8,13},{9,14},{10,15},{16,21},{17,22},{18,23},{2... | collective-permute-start | bytes 6291464 | tf_op jit(solution)/shard_map/ppermute | solution.py:16
  609.1 6.2 copy-start.5
  632.3 12.6 %collective-permute-start.24 = (bf16[1,1,512,512]{2,3,1,0:T(8,128)(2,1)S(1)}, bf16[1,1,512,512]{2,3,1,0:T(8,128)(2,1)S(1)}, u32[]{:S(2)}, u32[]{:S(2)}) collective-permute-start(bf16[1,1,512,512]{2,3,1,0:T(8,128)(2,1)S(1)} %fusion.21), channel_id=1, source_target_pairs={{0,8},{8,16},{16,24},{1,9},{9,17},{17,25},{2,10},{10,18},{18,26},{... | collective-permute-start | bytes 1572872 | tf_op jit(solution)/shard_map/ppermute | solution.py:27
  635.4 22.3 %collective-permute-start.25 = (bf16[1,1,512,512]{2,3,1,0:T(8,128)(2,1)S(1)}, bf16[1,1,512,512]{2,3,1,0:T(8,128)(2,1)S(1)}, u32[]{:S(2)}, u32[]{:S(2)}) collective-permute-start(bf16[1,1,512,512]{2,3,1,0:T(8,128)(2,1)S(1)} %fusion.21), channel_id=1, source_target_pairs={{8,0},{16,8},{24,16},{9,1},{17,9},{25,17},{10,2},{18,10},{26,18},{... | collective-permute-start | bytes 1572872 | tf_op jit(solution)/shard_map/ppermute | solution.py:29
  (58 other events, 309.8 us)
where the time goes:
time: 718 us; the launch traced here: 707 us
  local copies, waits for them, and re-layouts  428 us (60%)
  starting transfers between devices  105 us (15%)
  waiting for transfers between devices  77.8 us (11%)
  other arithmetic  53.7 us (7%)
  between operations  42.5 us (6%)
    gather x72, local copies, waits for them, and re-layouts, apply_taps(): picked = jnp.take(flipped, col_first + tap, axis=0).astype(jnp.float32)  209 us
    gather x72, local copies, waits for them, and re-layouts, apply_taps(): picked = jnp.take(window, row_first + tap, axis=0).astype(jnp.float32)  143 us
    ppermute x24, starting transfers between devices, from_behind(): return lax.ppermute(value, axis, pairs)  101 us
    ppermute x24, waiting for transfers between devices, from_behind(): return lax.ppermute(value, axis, pairs)  57.8 us
    broadcast_in_dim x1, other arithmetic, per_device(): blended = (numer / denom).astype(jnp.bfloat16)[:, None]  16.6 us
    gather x9, local copies, waits for them, and re-layouts, apply_taps(): window = lax.dynamic_slice(tile, (corner[0], corner[1]), (band, band))  15.3 us
    transpose x9, other arithmetic, apply_taps(): flipped = rows.astype(jnp.bfloat16).T  14.6 us
  transfers between devices with their start and end apart: 26, of which 6 were waited for; matrix products, arithmetic and copies ran while one was open for 53% of the time, Pallas kernels for 0%

commit v1 on v0

v1 whole, which is shorter than its diff:
```python
import functools

import jax
import jax.numpy as jnp
from jax import lax
from jax.experimental import pallas as pl
from jax.experimental.pallas import tpu as pltpu
from jax.sharding import PartitionSpec as P

BAND = 640
GY = 4
TAPS = 4
LANE = 128
WIN = BAND + LANE
EXTRA = 16
VMEM_LIMIT = 40 * 1024 * 1024

bf16 = jnp.bfloat16
f32 = jnp.float32


def vmem():
    return pl.BlockSpec(memory_space=pltpu.VMEM)


def smem():
    return pl.BlockSpec(memory_space=pltpu.SMEM)


def hbm():
    return pl.BlockSpec(memory_space=pltpu.HBM)


def params():
    return pltpu.CompilerParams(vmem_limit_bytes=VMEM_LIMIT)


def cost(flops, nbytes):
    return pl.CostEstimate(flops=int(flops), bytes_accessed=int(nbytes), transcendentals=0)


def slot_of(column, role, step):
    odd = column % 2
    if role == 0:
        across = 0
    elif role == 1:
        across = 1 - 2 * odd
    else:
        across = 2 * odd - 1
    return 3 * (across + 1) + (step + 1)


def my_column():
    return lax.rem(lax.axis_index("blk"), GY)


def my_row():
    return lax.div(lax.axis_index("blk"), GY)


def step_of(move):
    if move == "swap":
        return 1 - 2 * my_row()
    return -move


def pack_kernel(moves, rt_ref, ct_ref, rs_ref, cs_ref, foot_ref, off_ref, fr_ref, fc_ref, tile_ref, *refs):
    outs, (buf, fbuf, sems) = refs[:-3], refs[-3:]
    ext_ref, packed = outs[0], outs[1:]
    size = tile_ref.shape[0]
    whole = pltpu.make_async_copy(tile_ref, ext_ref.at[pl.ds(0, size)], sems.at[0])
    whole.start()
    edge = fr_ref.shape[1]
    fbuf[...] = jnp.zeros(fbuf.shape, bf16)
    fbuf[0:1, 0:edge] = fr_ref[...]
    fbuf[0:1, edge : 2 * edge] = fc_ref[...]
    tail = pltpu.make_async_copy(fbuf, ext_ref.at[pl.ds(size, EXTRA)], sems.at[1])
    tail.start()
    column = my_column()
    most = (size - BAND) // LANE - 1
    steps = [0] + [step_of(move) for move in moves]
    for group, step in enumerate(steps):
        for role in range(3):
            k = jnp.clip(slot_of(column, role, step), 0, 8)
            used = foot_ref[k].astype(f32)
            buf[0:TAPS] = rt_ref[k].astype(f32)
            buf[TAPS : 2 * TAPS] = ct_ref[k].astype(f32) * used
            for dim, ref in enumerate((rs_ref, cs_ref)):
                off = off_ref[2 * k + dim]
                base = jnp.minimum(lax.div(off, LANE), most)
                rel = ref[pl.ds(k, 1), :] + (off - base * LANE)
                high = lax.shift_right_logical(rel, 5)
                buf[8 + 2 * dim : 9 + 2 * dim] = high.astype(f32)
                buf[9 + 2 * dim : 10 + 2 * dim] = (rel - high * 32).astype(f32)
                buf[12 + dim : 13 + dim] = jnp.zeros((1, edge), f32) + base.astype(f32)
            buf[14:16] = jnp.zeros((2, edge), f32)
            packed[group][role] = buf[...].astype(bf16)
    whole.wait()
    tail.wait()


def pack(moves, rt, ct, rs, cs, foot, off, fr, fc, tile):
    size, edge = tile.shape[0], rs.shape[1]
    groups = 1 + len(moves)
    return pl.pallas_call(
        functools.partial(pack_kernel, moves),
        name="pack",
        out_shape=[jax.ShapeDtypeStruct((size + EXTRA, tile.shape[1]), bf16)]
        + [jax.ShapeDtypeStruct((3, 16, edge), bf16)] * groups,
        in_specs=[vmem()] * 4 + [smem()] * 2 + [vmem()] * 2 + [hbm()],
        out_specs=[hbm()] + [vmem()] * groups,
        scratch_shapes=[
            pltpu.VMEM((16, edge), f32),
            pltpu.VMEM((EXTRA, tile.shape[1]), bf16),
            pltpu.SemaphoreType.DMA((2,)),
        ],
        compiler_params=params(),
        cost_estimate=cost(1e6, 5e6),
    )(rt, ct, rs, cs, foot, off, fr, fc, tile)


def row_matrix(prm, edge):
    cols = prm.T
    rel = cols[:, 8:9] * 32.0 + cols[:, 9:10]
    rel = jnp.broadcast_to(rel, (edge, LANE))
    taps = [jnp.broadcast_to(cols[:, q : q + 1], (edge, LANE)).astype(bf16) for q in range(TAPS)]
    lane = lax.broadcasted_iota(jnp.int32, (edge, LANE), 1).astype(f32)
    parts = []
    for h in range(WIN // LANE):
        place = ((lane + float(LANE * h)) - rel).astype(bf16)
        part = jnp.zeros((edge, LANE), bf16)
        for q in range(TAPS):
            part = jnp.where(place == bf16(q), taps[q], part)
        parts.append(part)
    return jnp.concatenate(parts, axis=1)


def col_matrix(prm, edge):
    rel = prm[10:11] * 32.0 + prm[11:12]
    taps = [jnp.broadcast_to(prm[TAPS + q : TAPS + q + 1], (LANE, edge)).astype(bf16) for q in range(TAPS)]
    sub = lax.broadcasted_iota(jnp.int32, (LANE, edge), 0).astype(f32)
    parts = []
    for h in range(WIN // LANE):
        place = (sub - (rel - float(LANE * h))).astype(bf16)
        part = jnp.zeros((LANE, edge), bf16)
        for q in range(TAPS):
            part = jnp.where(place == bf16(q), taps[q], part)
        parts.append(part)
    return jnp.concatenate(parts, axis=0)


def contrib_kernel(slots, only_middle, feather_row, prm_ref, *refs):
    count = len(slots)
    tiles, out_ref = refs[:count], refs[count]
    win, fth, sems = refs[count + 1 :]
    edge = out_ref.shape[1]
    size = tiles[0].shape[0] - EXTRA

    def work():
        copies = []
        for s, slot in enumerate(slots):
            base = prm_ref[slot].astype(f32)
            r0 = pl.multiple_of(jnp.max(base[12:13, 0:LANE]).astype(jnp.int32) * LANE, LANE)
            c0 = pl.multiple_of(jnp.max(base[13:14, 0:LANE]).astype(jnp.int32) * LANE, LANE)
            window = pltpu.make_async_copy(
                tiles[s].at[pl.ds(r0, WIN), pl.ds(c0, WIN)], win.at[s], sems.at[s, 0]
            )
            feather = pltpu.make_async_copy(tiles[s].at[pl.ds(size, EXTRA)], fth.at[s], sems.at[s, 1])
            window.start()
            feather.start()
            copies.append((window, feather))
        total = None
        profiles = []
        for s, slot in enumerate(slots):
            prm = prm_ref[slot].astype(f32)
            rmat = row_matrix(prm, edge)
            cmat = col_matrix(prm, edge)
            copies[s][0].wait()
            copies[s][1].wait()
            rows = jnp.dot(rmat, win[s], preferred_element_type=f32).astype(bf16)
            contrib = jnp.dot(rows, cmat, preferred_element_type=f32)
            profile = fth[s].astype(f32)
            profiles += [profile[0:1, :edge], profile[0:1, edge:]]
            contrib = contrib * profile[:, :edge].T[:, 0:1] * profile[0:1, edge:]
            total = contrib if total is None else total + contrib
        out_ref[0:edge] = total.astype(out_ref.dtype)
        before = [jnp.zeros((feather_row, edge), f32)] if feather_row else []
        after = [jnp.zeros((EXTRA - feather_row - len(profiles), edge), f32)]
        out_ref[edge:] = jnp.concatenate(before + profiles + after, axis=0).astype(out_ref.dtype)

    if only_middle:
        column = my_column()
        pl.when(jnp.logical_and(column > 0, column < GY - 1))(work)
    else:
        work()


def contributions(name, prm, slots, tiles, edge, only_middle=False, feather_row=0):
    count = len(slots)
    return pl.pallas_call(
        functools.partial(contrib_kernel, slots, only_middle, feather_row),
        name=name,
        out_shape=jax.ShapeDtypeStruct((edge + EXTRA, edge), bf16),
        in_specs=[vmem()] + [hbm()] * count,
        out_specs=vmem(),
        scratch_shapes=[
            pltpu.VMEM((count, WIN, WIN), bf16),
            pltpu.VMEM((count, EXTRA, tiles[0].shape[1]), bf16),
            pltpu.SemaphoreType.DMA((count, 2)),
        ],
        compiler_params=params(),
        cost_estimate=cost(1.0e9 * count * 2, 1.2e6 * count + 5e5),
    )(prm, *tiles)


def weights_of(foot_ref, column, step, rows, roles):
    total = None
    cols = rows.T
    for role in roles:
        slot = slot_of(column, role, step)
        inside = jnp.logical_and(slot >= 0, slot < 9)
        used = jnp.where(inside, foot_ref[jnp.clip(slot, 0, 8)], 0).astype(f32)
        term = cols[:, 2 * role : 2 * role + 1] * (rows[2 * role + 1 : 2 * role + 2] * used)
        total = term if total is None else total + term
    return total


def same_row_kernel(foot_ref, own_ref, cross_ref, numer_ref, denom_ref):
    edge = own_ref.shape[1]
    rows = own_ref[edge:].astype(f32) + cross_ref[edge:].astype(f32)
    numer_ref[...] = own_ref[0:edge].astype(f32) + cross_ref[0:edge].astype(f32)
    denom_ref[...] = weights_of(foot_ref, my_column(), 0, rows, range(3))


def same_row(foot, own, cross, edge):
    return pl.pallas_call(
        same_row_kernel,
        name="same_row",
        out_shape=[jax.ShapeDtypeStruct((edge, edge), f32)] * 2,
        in_specs=[smem(), vmem(), vmem()],
        out_specs=[vmem(), vmem()],
        compiler_params=params(),
        cost_estimate=cost(4e6, 3e6),
    )(foot, own, cross)


def finish_kernel(moves, foot_ref, numer_ref, denom_ref, *refs):
    arrived, (blended_ref, pooled_ref, half) = refs[:-3], refs[-3:]
    edge = numer_ref.shape[0]
    numer, denom = numer_ref[...], denom_ref[...]
    for n, move in enumerate(moves):
        first, second = arrived[2 * n], arrived[2 * n + 1]
        numer = numer + (first[0:edge].astype(f32) + second[0:edge].astype(f32))
        rows = first[edge:].astype(f32) + second[edge:].astype(f32)
        denom = denom + weights_of(foot_ref, my_column(), step_of(move), rows, range(3))
    blended = (numer / denom).astype(bf16)
    blended_ref[...] = blended
    source = lax.broadcasted_iota(jnp.int32, (edge, edge // 2), 0)
    target = lax.broadcasted_iota(jnp.int32, (edge, edge // 2), 1)
    pairs = jnp.where(lax.shift_right_logical(source, 1) == target, 1.0, 0.0).astype(bf16)
    pooled = jnp.dot(blended, pairs, preferred_element_type=f32) * 0.25
    for h in range(edge // 2 // LANE):
        half[h] = pooled[:, h * LANE : (h + 1) * LANE]
        total = half[h, pl.ds(0, edge // 2, stride=2), :] + half[h, pl.ds(1, edge // 2, stride=2), :]
        pooled_ref[:, h * LANE : (h + 1) * LANE] = total.astype(bf16)


def finish(moves, foot, numer, denom, arrived, edge):
    return pl.pallas_call(
        functools.partial(finish_kernel, moves),
        name="finish",
        out_shape=[
            jax.ShapeDtypeStruct((edge, edge), bf16),
            jax.ShapeDtypeStruct((edge // 2, edge // 2), bf16),
        ],
        in_specs=[smem(), vmem(), vmem()] + [vmem()] * len(arrived),
        out_specs=[vmem(), vmem()],
        scratch_shapes=[pltpu.VMEM((edge // 2 // LANE, edge, LANE), f32)],
        compiler_params=params(),
        cost_estimate=cost(3e8, 4e6),
    )(foot, numer, denom, *arrived)


def per_device(
    tiles, row_taps, col_taps, row_starts, col_starts, feather_rows, feather_cols, footprint, offsets
):
    tile = tiles[0, 0]
    edge = row_starts.shape[3]
    devices = lax.axis_size("blk")
    rows = devices // GY
    moves = ["swap"] if rows == 2 else [1, -1]
    foot = footprint.reshape(9)

    def along(move, value, columns=range(GY), back=False):
        pairs = []
        for r in range(rows):
            to = (1 - r) if move == "swap" else r + (-move if back else move)
            if 0 <= to < rows:
                pairs += [(r * GY + c, to * GY + c) for c in columns]
        return lax.ppermute(value, "blk", pairs)

    def mate(value):
        return lax.ppermute(value, "blk", [(i, i ^ 1) for i in range(devices)])

    def cross(value):
        pairs = []
        for r in range(rows):
            for c in range(1, GY - 1, 2):
                pairs += [(r * GY + c, r * GY + c + 1), (r * GY + c + 1, r * GY + c)]
        return lax.ppermute(value, "blk", pairs)

    packed = pack(
        moves,
        row_taps[0, 0],
        col_taps[0, 0],
        row_starts[0, 0],
        col_starts[0, 0],
        foot,
        offsets.reshape(18),
        feather_rows[0],
        feather_cols[0],
        tile,
    )
    ext, own_prm, move_prm = packed[0], packed[1], packed[2:]
    ext_mate = mate(ext)
    asked = [along(move, prm, back=True) for move, prm in zip(moves, move_prm)]
    cross_prm = cross(jnp.stack([own_prm[2]] + [prm[2] for prm in asked]))
    arrived = []
    for n, move in enumerate(moves):
        over = contributions("cross_sum", cross_prm, [1 + n], [ext], edge, True, 4)
        over = cross(over)
        local = contributions("local_sum", asked[n], [0, 1], [ext, ext_mate], edge)
        arrived.append(along(move, local, [0, GY - 1]))
        arrived.append(along(move, local + over, range(1, GY - 1)))
    side = cross(contributions("cross_own", cross_prm, [0], [ext], edge, True, 4))
    own = contributions("local_own", own_prm, [0, 1], [ext, ext_mate], edge)
    numer, denom = same_row(foot, own, side, edge)
    blended, pooled = finish(moves, foot, numer, denom, arrived, edge)
    sections = lax.axis_size("sec")
    before = lax.ppermute(pooled, "sec", [(i, i + 1) for i in range(sections - 1)])
    after = lax.ppermute(pooled, "sec", [(i + 1, i) for i in range(sections - 1)])
    index = lax.axis_index("sec")
    present = 4.0 - (index == 0).astype(f32) - (index == sections - 1).astype(f32)
    level = (before.astype(f32) + 2.0 * pooled.astype(f32) + after.astype(f32)) / present
    return blended[None, None], level.astype(bf16)[None, None]


def solution(mesh):
    return jax.shard_map(
        per_device,
        mesh=mesh,
        in_specs=(
            P("sec", "blk", None, None),
            P("sec", "blk", None, None, None),
            P("sec", "blk", None, None, None),
            P("sec", "blk", None, None),
            P("sec", "blk", None, None),
            P("sec", "blk", None),
            P("sec", "blk", None),
            P("sec", "blk", None),
            P("sec", "blk", None, None),
        ),
        out_specs=(P("sec", "blk", None, None), P("sec", "blk", None, None)),
        check_vma=False,
    )
```

time: 718 us -> 69.7 us (0.10)
  the two profiles are of different devices: /device:TPU:1 before, /device:TPU:28 now
where the time goes in v1:
time: 69.7 us; the launch traced here: 69.2 us
  waiting for transfers between devices  25.6 us (37%)
  Pallas kernels  18.6 us (27%)
  starting transfers between devices  16.6 us (24%)
  local copies, waits for them, and re-layouts  6.75 us (10%)
  other arithmetic  0.88 us (1%)
  between operations  0.8 us (1%)
    pallas_call x4, Pallas kernels, contributions(): pl.pallas_call(functools.partial(contrib_kernel, slots, only_middle, feat...  14.5 us
    ppermute x3, waiting for transfers between devices, along(): return lax.ppermute(value, 'blk', pairs)  14.1 us
    ppermute x3, starting transfers between devices, cross(): return lax.ppermute(value, 'blk', pairs)  7.49 us
    unnamed x16, local copies, waits for them, and re-layouts  6.66 us
    ppermute x3, waiting for transfers between devices, cross(): return lax.ppermute(value, 'blk', pairs)  6.24 us
    ppermute x1, waiting for transfers between devices, per_device(): lax.ppermute(pooled, 'sec', [(i, i + 1) for i in range(sections - 1)])  4.25 us
    ppermute x1, starting transfers between devices, per_device(): lax.ppermute(pooled, 'sec', [(i + 1, i) for i in range(sections - 1)])  3.33 us
    ppermute x3, starting transfers between devices, along(): return lax.ppermute(value, 'blk', pairs)  3.2 us
  transfers between devices with their start and end apart: 9, of which 6 were waited for; matrix products, arithmetic and copies ran while one was open for 0% of the time, Pallas kernels for 23%

profile of v1, /device:TPU:28, one launch (start us, length us, event | category | flops | bytes accessed | tf_op | source)
XLA Modules:
  0.0 69.2 jit_solution(16114034956741054431)
XLA Ops:
  0.6 0.8 %copy.12 = s32[1,1,9,2]{3,2,1,0:T(8,128)S(1)} copy(s32[1,1,9,2]{2,3,1,0:T(2,128)} %param.17) | data formatting | bytes 144 | tf_op args[8]
  1.4 0.1 reshape.11.off_ref
  1.5 0.7 %copy_bitcast_fusion = (s32[9,512]{1,0:T(8,128)S(1)}, s32[9,512]{1,0:T(8,128)S(1)}) fusion(s32[1,1,9,512]{3,1,2,0:T(1,128)} %param.13, s32[1,1,9,512]{3,1,2,0:T(1,128)} %param.12), kind=kLoop, calls=%fused_computation.3 | loop fusion | bytes 73728
  2.2 1.6 %copy-done = bf16[1,1,1024,1024]{3,2,1,0:T(8,128)(2,1)S(1)} copy-done((bf16[1,1,1024,1024]{3,2,1,0:T(8,128)(2,1)S(1)}, bf16[1,1,1024,1024]{3,2,1,0:T(8,128)(2,1)}, u32[]{:S(2)}) %copy-start) | copy-done | bytes 2097176
  3.8 0.8 %copy-done.1 = bf16[1,1,9,4,512]{4,3,2,1,0:T(4,128)(2,1)S(1)} copy-done((bf16[1,1,9,4,512]{4,3,2,1,0:T(4,128)(2,1)S(1)}, bf16[1,1,9,4,512]{4,3,2,1,0:T(4,128)(2,1)}, u32[]{:S(2)}) %copy-start.1) | copy-done | bytes 36888
  4.6 0.8 %copy-done.2 = bf16[1,1,9,4,512]{4,3,2,1,0:T(4,128)(2,1)S(1)} copy-done((bf16[1,1,9,4,512]{4,3,2,1,0:T(4,128)(2,1)S(1)}, bf16[1,1,9,4,512]{4,3,2,1,0:T(4,128)(2,1)}, u32[]{:S(2)}) %copy-start.2) | copy-done | bytes 36888
  5.4 0.7 copy-done.3
  6.0 0.7 copy-done.5
  6.7 0.7 copy-done.6
  7.4 0.9 %pack.1 = (bf16[1040,1024]{1,0:T(8,128)(2,1)S(1)}, bf16[3,16,512]{2,1,0:T(8,128)(2,1)S(1)}, bf16[3,16,512]{2,1,0:T(8,128)(2,1)S(1)}) custom-call(bf16[9,4,512]{2,1,0:T(4,128)(2,1)S(1)} %bitcast.14, bf16[9,4,512]{2,1,0:T(4,128)(2,1)S(1)} %bitcast.15, s32[9,512]{1,0:T(8,128)S(1)} %get-tuple-element.17.rs_ref, s32[9,512]{1,0:T(8,128)S(1)} %get-tuple-element.16.cs_ref, ...), custom_call_target="tpu_custom_call" | custom-call | flops 1000000 | bytes 5000000 | tf_op jit(solution)/shard_map/pack/pallas_call | solution.py:105
  8.3 0.4 collective-permute-start.1
  8.7 5.6 %collective-permute-done.1.prm_ref = bf16[3,16,512]{2,1,0:T(8,128)(2,1)S(1)} collective-permute-done((bf16[3,16,512]{2,1,0:T(8,128)(2,1)S(1)}, bf16[3,16,512]{2,1,0:T(8,128)(2,1)S(1)}, u32[]{:S(2)}, u32[]{:S(2)}) %collective-permute-start.1) | collective-permute-done | bytes 49184 | tf_op jit(solution)/shard_map/ppermute | solution.py:300
  14.3 1.9 %collective-permute-start.2 = (bf16[2,16,512]{2,1,0:T(8,128)(2,1)S(1)}, bf16[2,16,512]{2,1,0:T(8,128)(2,1)S(1)}, u32[]{:S(2)}, u32[]{:S(2)}) collective-permute-start(bf16[2,16,512]{2,1,0:T(8,128)(2,1)S(1)} %pad_maximum_fusion), channel_id=1, source_target_pairs={{1,2},{2,1},{5,6},{6,5},{9,10},{10,9},{13,14},{14,13},{17,18},{18,... | collective-permute-start | bytes 98312 | tf_op jit(solution)/shard_map/ppermute | solution.py:310
  16.3 3.3 %collective-permute-done.2.prm_ref = bf16[2,16,512]{2,1,0:T(8,128)(2,1)S(1)} collective-permute-done((bf16[2,16,512]{2,1,0:T(8,128)(2,1)S(1)}, bf16[2,16,512]{2,1,0:T(8,128)(2,1)S(1)}, u32[]{:S(2)}, u32[]{:S(2)}) %collective-permute-start.2) | collective-permute-done | bytes 32800 | tf_op jit(solution)/shard_map/ppermute | solution.py:310
  19.6 2.5 %cross_sum.1 = bf16[528,512]{1,0:T(8,128)(2,1)S(1)} custom-call(bf16[2,16,512]{2,1,0:T(8,128)(2,1)S(1)} %collective-permute-done.2.prm_ref, bf16[1040,1024]{1,0:T(8,128)(2,1)S(1)} %get-tuple-element.10.refs_0_), custom_call_target="tpu_custom_call" | custom-call | flops 2000000000 | bytes 1700000 | tf_op jit(solution)/shard_map/cross_sum/pallas_call | solution.py:200
  22.0 1.9 %collective-permute-start.5 = (bf16[528,512]{1,0:T(8,128)(2,1)S(1)}, bf16[528,512]{1,0:T(8,128)(2,1)S(1)}, u32[]{:S(2)}, u32[]{:S(2)}) collective-permute-start(bf16[528,512]{1,0:T(8,128)(2,1)S(1)} %cross_sum.1), channel_id=1, source_target_pairs={{1,2},{2,1},{5,6},{6,5},{9,10},{10,9},{13,14},{14,13},{17,18},{18,... | collective-permute-start | bytes 1622024 | tf_op jit(solution)/shard_map/ppermute | solution.py:310
  24.0 2.5 %cross_own.1 = bf16[528,512]{1,0:T(8,128)(2,1)S(1)} custom-call(bf16[2,16,512]{2,1,0:T(8,128)(2,1)S(1)} %collective-permute-done.2.prm_ref, bf16[1040,1024]{1,0:T(8,128)(2,1)S(1)} %get-tuple-element.10.refs_0_), custom_call_target="tpu_custom_call" | custom-call | flops 2000000000 | bytes 1700000 | tf_op jit(solution)/shard_map/cross_own/pallas_call | solution.py:200
  26.5 3.6 %collective-permute-start.3 = (bf16[528,512]{1,0:T(8,128)(2,1)S(1)}, bf16[528,512]{1,0:T(8,128)(2,1)S(1)}, u32[]{:S(2)}, u32[]{:S(2)}) collective-permute-start(bf16[528,512]{1,0:T(8,128)(2,1)S(1)} %cross_own.1), channel_id=1, source_target_pairs={{1,2},{2,1},{5,6},{6,5},{9,10},{10,9},{13,14},{14,13},{17,18},{18,... | collective-permute-start | bytes 1622024 | tf_op jit(solution)/shard_map/ppermute | solution.py:310
  30.1 4.8 %local_sum.1 = bf16[528,512]{1,0:T(8,128)(2,1)S(1)} custom-call(bf16[3,16,512]{2,1,0:T(8,128)(2,1)S(1)} %collective-permute-done.1.prm_ref, bf16[1040,1024]{1,0:T(8,128)(2,1)S(1)} %get-tuple-element.10.refs_0_, bf16[1040,1024]{1,0:T(8,128)(2,1)S(1)} %collective-permute-done.refs_1_), custom_call_target="tpu_custom_call" | custom-call | flops 4000000000 | bytes 2900000 | tf_op jit(solution)/shard_map/local_sum/pallas_call | solution.py:200
  34.9 2.9 %collective-permute-done.5 = bf16[528,512]{1,0:T(8,128)(2,1)S(1)} collective-permute-done((bf16[528,512]{1,0:T(8,128)(2,1)S(1)}, bf16[528,512]{1,0:T(8,128)(2,1)S(1)}, u32[]{:S(2)}, u32[]{:S(2)}) %collective-permute-start.5) | collective-permute-done | bytes 540704 | tf_op jit(solution)/shard_map/ppermute | solution.py:310
  37.8 0.1 add.9
  38.0 1.9 %collective-permute-start.6 = (bf16[528,512]{1,0:T(8,128)(2,1)S(1)}, bf16[528,512]{1,0:T(8,128)(2,1)S(1)}, u32[]{:S(2)}, u32[]{:S(2)}) collective-permute-start(bf16[528,512]{1,0:T(8,128)(2,1)S(1)} %add.9), channel_id=1, source_target_pairs={{1,5},{2,6},{5,1},{6,2},{9,13},{10,14},{13,9},{14,10},{17,21},{18,... | collective-permute-start | bytes 1622024 | tf_op jit(solution)/shard_map/ppermute | solution.py:300
  39.9 0.9 %collective-permute-start.4 = (bf16[528,512]{1,0:T(8,128)(2,1)S(1)}, bf16[528,512]{1,0:T(8,128)(2,1)S(1)}, u32[]{:S(2)}, u32[]{:S(2)}) collective-permute-start(bf16[528,512]{1,0:T(8,128)(2,1)S(1)} %local_sum.1), channel_id=1, source_target_pairs={{0,4},{3,7},{4,0},{7,3},{8,12},{11,15},{12,8},{15,11},{16,20},{19,... | collective-permute-start | bytes 1622024 | tf_op jit(solution)/shard_map/ppermute | solution.py:300
  40.8 4.8 %local_own.1.own_ref = bf16[528,512]{1,0:T(8,128)(2,1)S(1)} custom-call(bf16[3,16,512]{2,1,0:T(8,128)(2,1)S(1)} %get-tuple-element.9.prm_ref, bf16[1040,1024]{1,0:T(8,128)(2,1)S(1)} %get-tuple-element.10.refs_0_, bf16[1040,1024]{1,0:T(8,128)(2,1)S(1)} %collective-permute-done.refs_1_), custom_call_target="tpu_custom_call" | custom-call | flops 4000000000 | bytes 2900000 | tf_op jit(solution)/shard_map/local_own/pallas_call | solution.py:200
  45.6 1.1 %same_row.1 = (f32[512,512]{1,0:T(8,128)S(1)}, f32[512,512]{1,0:T(8,128)S(1)}) custom-call(s32[9]{0:T(128)S(1)} %bitcast.17, bf16[528,512]{1,0:T(8,128)(2,1)S(1)} %local_own.1.own_ref, bf16[528,512]{1,0:T(8,128)(2,1)S(1)} %collective-permute-done.3.cross_ref), custom_call_target="tpu_custom_call" | custom-call | flops 4000000 | bytes 3000000 | tf_op jit(solution)/shard_map/same_row/pallas_call | solution.py:236
  46.7 8.6 %collective-permute-done.6.refs_1_ = bf16[528,512]{1,0:T(8,128)(2,1)S(1)} collective-permute-done((bf16[528,512]{1,0:T(8,128)(2,1)S(1)}, bf16[528,512]{1,0:T(8,128)(2,1)S(1)}, u32[]{:S(2)}, u32[]{:S(2)}) %collective-permute-start.6) | collective-permute-done | bytes 540704 | tf_op jit(solution)/shard_map/ppermute | solution.py:300
  55.3 2.1 %finish.1 = (bf16[512,512]{1,0:T(8,128)(2,1)}, bf16[256,256]{1,0:T(8,128)(2,1)S(1)}) custom-call(s32[9]{0:T(128)S(1)} %bitcast.18, f32[512,512]{1,0:T(8,128)S(1)} %get-tuple-element.12.numer_ref, f32[512,512]{1,0:T(8,128)S(1)} %get-tuple-element.13.denom_ref, bf16[528,512]{1,0:T(8,128)(2,1)S(1)} %collective-permute-done.4.refs_0_, ...), custom_call_target="tpu_custom_call" | custom-call | flops 300000000 | bytes 4000000 | tf_op jit(solution)/shard_map/finish/pallas_call | solution.py:269
  57.4 3.3 %collective-permute-start.8 = (bf16[256,256]{1,0:T(8,128)(2,1)S(1)}, bf16[256,256]{1,0:T(8,128)(2,1)S(1)}, u32[]{:S(2)}, u32[]{:S(2)}) collective-permute-start(bf16[256,256]{1,0:T(8,128)(2,1)S(1)} %get-tuple-element.15), channel_id=1, source_target_pairs={{8,0},{16,8},{24,16},{9,1},{17,9},{25,17},{10,2},{18,10},{26,18},{... | collective-permute-start | bytes 393224 | tf_op jit(solution)/shard_map/ppermute | solution.py:341
  60.7 2.5 %collective-permute-start.7 = (bf16[256,256]{1,0:T(8,128)(2,1)S(1)}, bf16[256,256]{1,0:T(8,128)(2,1)S(1)}, u32[]{:S(2)}, u32[]{:S(2)}) collective-permute-start(bf16[256,256]{1,0:T(8,128)(2,1)S(1)} %get-tuple-element.15), channel_id=1, source_target_pairs={{0,8},{8,16},{16,24},{1,9},{9,17},{17,25},{2,10},{10,18},{18,26},{... | collective-permute-start | bytes 393224 | tf_op jit(solution)/shard_map/ppermute | solution.py:340
  63.2 1.0 %collective-permute-done.8 = bf16[256,256]{1,0:T(8,128)(2,1)S(1)} collective-permute-done((bf16[256,256]{1,0:T(8,128)(2,1)S(1)}, bf16[256,256]{1,0:T(8,128)(2,1)S(1)}, u32[]{:S(2)}, u32[]{:S(2)}) %collective-permute-start.8) | collective-permute-done | bytes 131104 | tf_op jit(solution)/shard_map/ppermute | solution.py:341
  64.2 4.2 %collective-permute-done.7 = bf16[256,256]{1,0:T(8,128)(2,1)S(1)} collective-permute-done((bf16[256,256]{1,0:T(8,128)(2,1)S(1)}, bf16[256,256]{1,0:T(8,128)(2,1)S(1)}, u32[]{:S(2)}, u32[]{:S(2)}) %collective-permute-start.7) | collective-permute-done | bytes 131104 | tf_op jit(solution)/shard_map/ppermute | solution.py:340
  68.5 0.7 %fusion = bf16[1,1,256,256]{3,2,1,0:T(8,128)(2,1)} fusion(f32[]{:T(128)S(6)} %sub.7, bf16[256,256]{1,0:T(8,128)(2,1)S(1)} %collective-permute-done.8, bf16[256,256]{1,0:T(8,128)(2,1)S(1)} %get-tuple-element.15, bf16[256,256]{1,0:T(8,128)(2,1)S(1)} %collective-permute-done.7), kind=kLoop, calls=%fused_computation.1 | loop fusion | flops 524288 | bytes 524292 | tf_op jit(solution)/shard_map/broadcast_in_dim | solution.py:345
  (15 shorter events, 0.1 us)
Async XLA Ops:
  2.2 1.6 %copy-start = (bf16[1,1,1024,1024]{3,2,1,0:T(8,128)(2,1)S(1)}, bf16[1,1,1024,1024]{3,2,1,0:T(8,128)(2,1)}, u32[]{:S(2)}) copy-start(bf16[1,1,1024,1024]{3,2,1,0:T(8,128)(2,1)} %param.9) | copy-start | bytes 6291460
  3.8 0.8 %copy-start.1 = (bf16[1,1,9,4,512]{4,3,2,1,0:T(4,128)(2,1)S(1)}, bf16[1,1,9,4,512]{4,3,2,1,0:T(4,128)(2,1)}, u32[]{:S(2)}) copy-start(bf16[1,1,9,4,512]{4,3,2,1,0:T(4,128)(2,1)} %param.10) | copy-start | bytes 110596
  4.6 0.8 %copy-start.2 = (bf16[1,1,9,4,512]{4,3,2,1,0:T(4,128)(2,1)S(1)}, bf16[1,1,9,4,512]{4,3,2,1,0:T(4,128)(2,1)}, u32[]{:S(2)}) copy-start(bf16[1,1,9,4,512]{4,3,2,1,0:T(4,128)(2,1)} %param.11) | copy-start | bytes 110596
  5.4 0.7 copy-start.3
  6.0 0.7 copy-start.5
  6.7 0.7 copy-start.6
  8.2 21.9 %collective-permute-start = (bf16[1040,1024]{1,0:T(8,128)(2,1)S(1)}, bf16[1040,1024]{1,0:T(8,128)(2,1)S(1)}, u32[]{:S(2)}, u32[]{:S(2)}) collective-permute-start(bf16[1040,1024]{1,0:T(8,128)(2,1)S(1)} %get-tuple-element.10.refs_0_), channel_id=1, source_target_pairs={{0,1},{1,0},{2,3},{3,2},{4,5},{5,4},{6,7},{7,6},{8,9},{9,8},{10,11... | collective-permute-start | bytes 6389768 | tf_op jit(solution)/shard_map/ppermute | solution.py:303
  8.3 6.0 %collective-permute-start.1 = (bf16[3,16,512]{2,1,0:T(8,128)(2,1)S(1)}, bf16[3,16,512]{2,1,0:T(8,128)(2,1)S(1)}, u32[]{:S(2)}, u32[]{:S(2)}) collective-permute-start(bf16[3,16,512]{2,1,0:T(8,128)(2,1)S(1)} %get-tuple-element.11), channel_id=1, source_target_pairs={{0,4},{1,5},{2,6},{3,7},{4,0},{5,1},{6,2},{7,3},{8,12},{9,13},{10,... | collective-permute-start | bytes 147464 | tf_op jit(solution)/shard_map/ppermute | solution.py:300
  14.3 5.2 %collective-permute-start.2 = (bf16[2,16,512]{2,1,0:T(8,128)(2,1)S(1)}, bf16[2,16,512]{2,1,0:T(8,128)(2,1)S(1)}, u32[]{:S(2)}, u32[]{:S(2)}) collective-permute-start(bf16[2,16,512]{2,1,0:T(8,128)(2,1)S(1)} %pad_maximum_fusion), channel_id=1, source_target_pairs={{1,2},{2,1},{5,6},{6,5},{9,10},{10,9},{13,14},{14,13},{17,18},{18,... | collective-permute-start | bytes 98312 | tf_op jit(solution)/shard_map/ppermute | solution.py:310
  22.0 15.8 %collective-permute-start.5 = (bf16[528,512]{1,0:T(8,128)(2,1)S(1)}, bf16[528,512]{1,0:T(8,128)(2,1)S(1)}, u32[]{:S(2)}, u32[]{:S(2)}) collective-permute-start(bf16[528,512]{1,0:T(8,128)(2,1)S(1)} %cross_sum.1), channel_id=1, source_target_pairs={{1,2},{2,1},{5,6},{6,5},{9,10},{10,9},{13,14},{14,13},{17,18},{18,... | collective-permute-start | bytes 1622024 | tf_op jit(solution)/shard_map/ppermute | solution.py:310
  26.5 19.1 %collective-permute-start.3 = (bf16[528,512]{1,0:T(8,128)(2,1)S(1)}, bf16[528,512]{1,0:T(8,128)(2,1)S(1)}, u32[]{:S(2)}, u32[]{:S(2)}) collective-permute-start(bf16[528,512]{1,0:T(8,128)(2,1)S(1)} %cross_own.1), channel_id=1, source_target_pairs={{1,2},{2,1},{5,6},{6,5},{9,10},{10,9},{13,14},{14,13},{17,18},{18,... | collective-permute-start | bytes 1622024 | tf_op jit(solution)/shard_map/ppermute | solution.py:310
  38.0 7.6 %copy-start.4 = (s32[1,1,9]{2,1,0:T(1,128)S(1)}, s32[1,1,9]{2,1,0:T(1,128)}, u32[]{:S(2)}) copy-start(s32[1,1,9]{2,1,0:T(1,128)} %param.16) | copy-start | bytes 112
  38.0 17.3 %collective-permute-start.6 = (bf16[528,512]{1,0:T(8,128)(2,1)S(1)}, bf16[528,512]{1,0:T(8,128)(2,1)S(1)}, u32[]{:S(2)}, u32[]{:S(2)}) collective-permute-start(bf16[528,512]{1,0:T(8,128)(2,1)S(1)} %add.9), channel_id=1, source_target_pairs={{1,5},{2,6},{5,1},{6,2},{9,13},{10,14},{13,9},{14,10},{17,21},{18,... | collective-permute-start | bytes 1622024 | tf_op jit(solution)/shard_map/ppermute | solution.py:300
  39.9 15.4 %collective-permute-start.4 = (bf16[528,512]{1,0:T(8,128)(2,1)S(1)}, bf16[528,512]{1,0:T(8,128)(2,1)S(1)}, u32[]{:S(2)}, u32[]{:S(2)}) collective-permute-start(bf16[528,512]{1,0:T(8,128)(2,1)S(1)} %local_sum.1), channel_id=1, source_target_pairs={{0,4},{3,7},{4,0},{7,3},{8,12},{11,15},{12,8},{15,11},{16,20},{19,... | collective-permute-start | bytes 1622024 | tf_op jit(solution)/shard_map/ppermute | solution.py:300
  57.4 6.8 %collective-permute-start.8 = (bf16[256,256]{1,0:T(8,128)(2,1)S(1)}, bf16[256,256]{1,0:T(8,128)(2,1)S(1)}, u32[]{:S(2)}, u32[]{:S(2)}) collective-permute-start(bf16[256,256]{1,0:T(8,128)(2,1)S(1)} %get-tuple-element.15), channel_id=1, source_target_pairs={{8,0},{16,8},{24,16},{9,1},{17,9},{25,17},{10,2},{18,10},{26,18},{... | collective-permute-start | bytes 393224 | tf_op jit(solution)/shard_map/ppermute | solution.py:341
  60.7 7.8 %collective-permute-start.7 = (bf16[256,256]{1,0:T(8,128)(2,1)S(1)}, bf16[256,256]{1,0:T(8,128)(2,1)S(1)}, u32[]{:S(2)}, u32[]{:S(2)}) collective-permute-start(bf16[256,256]{1,0:T(8,128)(2,1)S(1)} %get-tuple-element.15), channel_id=1, source_target_pairs={{0,8},{8,16},{16,24},{1,9},{9,17},{17,25},{2,10},{10,18},{18,26},{... | collective-permute-start | bytes 393224 | tf_op jit(solution)/shard_map/ppermute | solution.py:340

commit v2 on v1

--- a/solution.py
+++ b/solution.py
@@ -281,7 +281,7 @@
     )(foot, numer, denom, *arrived)
 
 
-def per_device(
+def general_device(
     tiles, row_taps, col_taps, row_starts, col_starts, feather_rows, feather_cols, footprint, offsets
 ):
     tile = tiles[0, 0]
@@ -345,6 +345,386 @@
     return blended[None, None], level.astype(bf16)[None, None]
 
 
+HALF = 12
+PROFILE = 24
+BESIDE = 26
+SCALARS = 28
+CORNER = 8
+ROWS = 32
+TILE = 1024
+PREPARE_VMEM = 40 * 1024 * 1024
+WORK_VMEM = 40 * 1024 * 1024
+
+
+def is_outer():
+    column = my_column()
+    return jnp.logical_or(column == 0, column == GY - 1)
+
+
+def prepare_kernel(rt_hbm, ct_hbm, rs_hbm, cs_hbm, foot_hbm, off_hbm, fr_hbm, fc_hbm, *refs):
+    outs = refs[:4]
+    rt_ref, ct_ref, rs_ref, cs_ref, fr_ref, fc_ref, foot_ref, off_ref, buf, sems = refs[4:]
+    pairs = [
+        (off_hbm, off_ref),
+        (foot_hbm, foot_ref),
+        (rt_hbm, rt_ref),
+        (ct_hbm, ct_ref),
+        (rs_hbm, rs_ref),
+        (cs_hbm, cs_ref),
+        (fr_hbm, fr_ref),
+        (fc_hbm, fc_ref),
+    ]
+    copies = [pltpu.make_async_copy(a, b, sems.at[i]) for i, (a, b) in enumerate(pairs)]
+    for copy in copies:
+        copy.start()
+    for copy in copies:
+        copy.wait()
+    edge = fr_ref.shape[1]
+    column = my_column()
+    over = 1 - 2 * my_row()
+    most = (TILE - BAND) // LANE - 1
+    lane = lax.broadcasted_iota(jnp.int32, (1, edge), 1)
+    scalars = jnp.zeros((1, edge), f32)
+    for n in range(6):
+        slot = slot_of(column, n % 3, 0 if n < 3 else over)
+        inside = jnp.logical_and(slot >= 0, slot < 9)
+        used = jnp.where(inside, foot_ref[0, jnp.clip(slot, 0, 8)], 0).astype(f32)
+        scalars = jnp.where(lane == n, used, scalars)
+
+    def message(out_ref, slots, profile_row):
+        row = scalars
+        buf[...] = jnp.zeros(buf.shape, f32)
+        for half, (role, step) in enumerate(slots):
+            k = jnp.clip(slot_of(column, role, step), 0, 8)
+            used = foot_ref[0, k].astype(f32)
+            at = half * HALF
+            buf[at : at + TAPS] = rt_ref[k].astype(f32)
+            buf[at + TAPS : at + 2 * TAPS] = ct_ref[k].astype(f32) * used
+            for dim, ref in enumerate((rs_ref, cs_ref)):
+                off = off_ref[dim, k]
+                base = jnp.minimum(lax.div(off, LANE), most)
+                rel = ref[k] + (off - base * LANE)
+                high = lax.shift_right_logical(rel, 5)
+                first = at + 2 * TAPS + 2 * dim
+                buf[first : first + 1] = high.astype(f32)
+                buf[first + 1 : first + 2] = (rel - high * 32).astype(f32)
+                row = jnp.where(lane == CORNER + 2 * half + dim, base.astype(f32), row)
+        buf[profile_row : profile_row + 1] = fr_ref[...].astype(f32)
+        buf[profile_row + 1 : profile_row + 2] = fc_ref[...].astype(f32)
+        buf[SCALARS : SCALARS + 1] = row
+        out_ref[...] = buf[...].astype(bf16)
+
+    message(outs[0], [(0, over), (1, over)], PROFILE)
+    message(outs[1], [(2, over)], PROFILE)
+    message(outs[2], [(2, 0)], BESIDE)
+    message(outs[3], [(0, 0), (1, 0)], PROFILE)
+
+
+def prepare(rt, ct, rs, cs, foot, off, fr, fc):
+    edge = fr.shape[1]
+    args = [pltpu.with_memory_space_constraint(x, pltpu.HBM) for x in (rt, ct, rs, cs, foot, off, fr, fc)]
+    return pl.pallas_call(
+        prepare_kernel,
+        name="prepare",
+        out_shape=[jax.ShapeDtypeStruct((ROWS, edge), bf16)] * 4,
+        in_specs=[hbm()] * 8,
+        out_specs=[vmem()] * 4,
+        scratch_shapes=[pltpu.VMEM(x.shape, x.dtype) for x in (rt, ct, rs, cs, fr, fc)]
+        + [pltpu.SMEM(x.shape, x.dtype) for x in (foot, off)]
+        + [pltpu.VMEM((ROWS, edge), f32), pltpu.SemaphoreType.DMA((8,))],
+        compiler_params=pltpu.CompilerParams(vmem_limit_bytes=PREPARE_VMEM),
+        cost_estimate=cost(1e6, 2e5),
+    )(*args)
+
+
+def fetch_kernel(tile_ref, out_ref, sems):
+    parts = sems.shape[0]
+    size = out_ref.shape[0] // parts
+    copies = [
+        pltpu.make_async_copy(tile_ref.at[pl.ds(n * size, size)], out_ref.at[pl.ds(n * size, size)], sems.at[n])
+        for n in range(parts)
+    ]
+    for copy in copies:
+        copy.start()
+    for copy in copies:
+        copy.wait()
+
+
+def fetch(tile):
+    return pl.pallas_call(
+        fetch_kernel,
+        name="fetch",
+        out_shape=pltpu.VMEM(tile.shape, tile.dtype),
+        in_specs=[hbm()],
+        out_specs=vmem(),
+        scratch_shapes=[pltpu.SemaphoreType.DMA((8,))],
+        compiler_params=pltpu.CompilerParams(vmem_limit_bytes=PREPARE_VMEM),
+        cost_estimate=cost(1e6, 4e6),
+    )(pltpu.with_memory_space_constraint(tile, pltpu.HBM))
+
+
+def scalar_of(msg, n):
+    lane = lax.broadcasted_iota(jnp.int32, (1, LANE), 1)
+    return jnp.sum(jnp.where(lane == n, msg[SCALARS : SCALARS + 1, 0:LANE], 0.0))
+
+
+def corner(msg, half):
+    r0 = pl.multiple_of(scalar_of(msg, CORNER + 2 * half).astype(jnp.int32) * LANE, LANE)
+    c0 = pl.multiple_of(scalar_of(msg, CORNER + 2 * half + 1).astype(jnp.int32) * LANE, LANE)
+    return pl.ds(r0, WIN), pl.ds(c0, WIN)
+
+
+def window_copy(msg, half, mate_ref, win, sem):
+    copy = pltpu.make_async_copy(mate_ref.at[corner(msg, half)], win, sem)
+    copy.start()
+    return copy
+
+
+def contribution(msg, half, profile, tile_ref, edge, copy=None):
+    prm = msg[half * HALF : half * HALF + HALF]
+    prm = jnp.concatenate([prm, profile, jnp.zeros((2, edge), f32)], axis=0)
+    rmat = row_matrix(prm, edge)
+    cmat = col_matrix(prm, edge)
+    if copy is None:
+        window = tile_ref[corner(msg, half)]
+    else:
+        copy.wait()
+        window = tile_ref[...]
+    rows = jnp.dot(rmat, window, preferred_element_type=f32).astype(bf16)
+    contrib = jnp.dot(rows, cmat, preferred_element_type=f32)
+    return contrib * prm.T[:, HALF : HALF + 1] * profile[1:2]
+
+
+def local_pair(msg, profile, beside, tile_ref, mate_ref, win, sem, edge):
+    copy = window_copy(msg, 1, mate_ref, win, sem)
+    total = contribution(msg, 0, profile, tile_ref, edge)
+    return total + contribution(msg, 1, beside, win, edge, copy)
+
+
+def weight_sum(msg, profiles):
+    edge = msg.shape[1]
+    lane = lax.broadcasted_iota(jnp.int32, (1, edge), 1)
+    pad = [jnp.zeros((16 - len(profiles), edge), f32)]
+    rows, cols = [], []
+    for n, profile in enumerate(profiles):
+        used = jnp.sum(jnp.where(lane == n, msg[SCALARS : SCALARS + 1], 0.0), axis=1, keepdims=True)
+        rows.append(profile[0:1])
+        cols.append(profile[1:2] * used)
+    rows = jnp.concatenate(rows + pad, axis=0)
+    cols = jnp.concatenate(cols + pad, axis=0)
+    return jnp.dot(rows.T.astype(bf16), cols.astype(bf16), preferred_element_type=f32)
+
+
+def pool(block, half):
+    edge = block.shape[0]
+    source = lax.broadcasted_iota(jnp.int32, (edge, edge // 2), 0)
+    target = lax.broadcasted_iota(jnp.int32, (edge, edge // 2), 1)
+    pairs = jnp.where(lax.shift_right_logical(source, 1) == target, 0.25, 0.0).astype(bf16)
+    sums = jnp.dot(block, pairs, preferred_element_type=f32)
+    parts = []
+    for h in range(edge // 2 // LANE):
+        half[h] = sums[:, h * LANE : (h + 1) * LANE]
+        parts.append(half[h, pl.ds(0, edge // 2, stride=2), :] + half[h, pl.ds(1, edge // 2, stride=2), :])
+    return jnp.concatenate(parts, axis=1)
+
+
+def behind(profile, edge):
+    return jnp.concatenate([profile, jnp.zeros((EXTRA - 2, edge), f32)], axis=0).astype(bf16)
+
+
+def own_profiles(mine_ref, theirs_ref):
+    mine, theirs = mine_ref[...].astype(f32), theirs_ref[...].astype(f32)
+    return mine[PROFILE : PROFILE + 2], theirs[BESIDE : BESIDE + 2]
+
+
+def first_kernel(got_ref, mine_ref, theirs_ref, tile_ref, mate_ref, out_ref, win, sem):
+    edge = out_ref.shape[1]
+    outer = is_outer()
+    profile, beside = own_profiles(mine_ref, theirs_ref)
+    msg = got_ref[...].astype(f32)
+
+    @pl.when(outer)
+    def _():
+        total = local_pair(msg, profile, beside, tile_ref, mate_ref, win, sem, edge)
+        none = jnp.zeros_like(profile)
+        theirs = [msg[PROFILE : PROFILE + 2], msg[BESIDE : BESIDE + 2], none]
+        denom = weight_sum(msg, theirs + [profile, beside, none])
+        out_ref[0:edge] = (total / denom).astype(bf16)
+        out_ref[edge:] = jnp.zeros((EXTRA, edge), bf16)
+
+    @pl.when(jnp.logical_not(outer))
+    def _():
+        out_ref[0:edge] = contribution(msg, 0, profile, tile_ref, edge).astype(bf16)
+        out_ref[edge:] = behind(profile, edge)
+
+
+def second_kernel(down_ref, mine_ref, theirs_ref, tile_ref, mate_ref, out_ref, win, sem):
+    edge = out_ref.shape[1]
+    outer = is_outer()
+    profile, beside = own_profiles(mine_ref, theirs_ref)
+    msg = down_ref[...].astype(f32)
+
+    @pl.when(outer)
+    def _():
+        copy = window_copy(msg, 0, mate_ref, win, sem)
+        out_ref[0:edge] = contribution(msg, 0, beside, win, edge, copy).astype(bf16)
+        out_ref[edge:] = behind(beside, edge)
+
+    @pl.when(jnp.logical_not(outer))
+    def _():
+        total = local_pair(msg, profile, beside, tile_ref, mate_ref, win, sem, edge)
+        out_ref[0:edge] = total.astype(bf16)
+        out_ref[edge:] = jnp.zeros((EXTRA, edge), bf16)
+
+
+def merge_kernel(local_ref, over_ref, got_ref, down_ref, mine_ref, theirs_ref, out_ref, pooled_ref, half):
+    edge = out_ref.shape[1]
+
+    @pl.when(jnp.logical_not(is_outer()))
+    def _():
+        profile, beside = own_profiles(mine_ref, theirs_ref)
+        msg = down_ref[...].astype(f32)
+        across = got_ref[...].astype(f32)[PROFILE : PROFILE + 2]
+        theirs = [msg[PROFILE : PROFILE + 2], msg[BESIDE : BESIDE + 2], across]
+        denom = weight_sum(msg, theirs + [profile, beside, over_ref[edge:].astype(f32)[0:2]])
+        total = local_ref[0:edge].astype(f32) + over_ref[0:edge].astype(f32)
+        block = (total / denom).astype(bf16)
+        out_ref[...] = block
+        pooled_ref[...] = pool(block, half).astype(bf16)
+
+
+def own_kernel(own_ref, mine_ref, theirs_ref, tile_ref, mate_ref, out_ref, win, sem):
+    profile, beside = own_profiles(mine_ref, theirs_ref)
+    msg = own_ref[...].astype(f32)
+    out_ref[...] = local_pair(msg, profile, beside, tile_ref, mate_ref, win, sem, out_ref.shape[1])
+
+
+def blend_kernel(
+    local_ref, side_ref, got_ref, down_ref, mine_ref, theirs_ref, early_ref, pooled_early_ref, out_ref, pooled_ref, half
+):
+    edge = out_ref.shape[1]
+    outer = is_outer()
+    profile, beside = own_profiles(mine_ref, theirs_ref)
+    got, down = got_ref[...].astype(f32), down_ref[...].astype(f32)
+    msg = jnp.where(outer, got, down)
+    theirs = [msg[PROFILE : PROFILE + 2], msg[BESIDE : BESIDE + 2], got[PROFILE : PROFILE + 2]]
+    mine_across = side_ref[edge:].astype(f32)[0:2]
+    denom = weight_sum(mine_ref[...].astype(f32), [profile, beside, mine_across] + theirs)
+    total = local_ref[...] + side_ref[0:edge].astype(f32)
+    early = jnp.where(outer, early_ref[0:edge].astype(f32), 0.0)
+    block = total / denom + early
+    out_ref[...] = block
+    pooled_ref[...] = (pool(block.astype(bf16), half) + pooled_early_ref[...].astype(f32)).astype(bf16)
+
+
+def last_kernel(block_ref, late_ref, out_ref):
+    out_ref[...] = (block_ref[...] + late_ref[...].astype(f32)).astype(bf16)
+
+
+def call(kernel, name, out_shape, operands, mate=None, halves=False, work=(1e9, 4e6)):
+    single = not isinstance(out_shape, list)
+    edge = (out_shape if single else out_shape[0]).shape[1]
+    scratch, far = [], []
+    if mate is not None:
+        scratch = [pltpu.VMEM((WIN, WIN), bf16), pltpu.SemaphoreType.DMA]
+        far = [pltpu.with_memory_space_constraint(mate, pltpu.HBM)]
+    if halves:
+        scratch = [pltpu.VMEM((edge // 2 // LANE, edge, LANE), f32)]
+    return pl.pallas_call(
+        kernel,
+        name=name,
+        out_shape=out_shape,
+        in_specs=[vmem()] * len(operands) + [hbm()] * len(far),
+        out_specs=vmem() if single else [vmem()] * len(out_shape),
+        scratch_shapes=scratch,
+        compiler_params=pltpu.CompilerParams(vmem_limit_bytes=WORK_VMEM),
+        cost_estimate=cost(*work),
+    )(*[pltpu.with_memory_space_constraint(x, pltpu.VMEM) for x in operands], *far)
+
+
+def two_row_device(
+    tiles, row_taps, col_taps, row_starts, col_starts, feather_rows, feather_cols, footprint, offsets
+):
+    tile = tiles[0, 0]
+    edge = row_starts.shape[3]
+    devices = lax.axis_size("blk")
+
+    def send(value, pairs):
+        return lax.ppermute(value, "blk", pairs)
+
+    def swap(pairs):
+        return [(i, j) for i, j in pairs] + [(j, i) for i, j in pairs]
+
+    in_chip = [(i, i ^ 1) for i in range(devices)]
+    vertical_outer = swap([(0, 4), (3, 7)])
+    vertical_inner = swap([(1, 5), (2, 6)])
+    diagonal = swap([(1, 6), (2, 5)])
+    across_inner = swap([(1, 2), (5, 6)])
+    across_outer = swap([(0, 3), (4, 7)])
+    outer_to_inner = [(0, 2), (3, 1), (4, 6), (7, 5)]
+
+    mine, diag, aside, own_msg = prepare(
+        row_taps[0, 0],
+        col_taps[0, 0],
+        row_starts.reshape(-1, 1, edge),
+        col_starts.reshape(-1, 1, edge),
+        footprint[0],
+        offsets[0, 0].T,
+        feather_rows[0],
+        feather_cols[0],
+    )
+    theirs = send(aside, in_chip)
+    theirs, tile_after = lax.optimization_barrier((theirs, tile))
+    mate = send(tile_after, in_chip)
+    near = fetch(tile)
+    outer = is_outer()
+    row = lax.broadcasted_iota(jnp.int32, mine.shape, 0)
+    from_beside = jnp.logical_and(row >= BESIDE, row < BESIDE + 2)
+    asking = jnp.where(from_beside, theirs, mine)
+    got = send(jnp.where(outer, asking, diag), vertical_outer + diagonal)
+    down = send(jnp.where(outer, theirs, asking), across_outer + vertical_inner)
+
+    block = jax.ShapeDtypeStruct((edge + EXTRA, edge), bf16)
+    bare = jax.ShapeDtypeStruct((edge, edge), bf16)
+    bare32 = jax.ShapeDtypeStruct((edge, edge), f32)
+    pooled = jax.ShapeDtypeStruct((edge // 2, edge // 2), bf16)
+    two = (4e9, 4e6)
+
+    got, down = lax.optimization_barrier((got, down))
+    first = call(first_kernel, "first", block, (got, mine, theirs, near), mate, work=two)
+    early = send(first, vertical_outer + across_inner)
+    second = call(second_kernel, "second", block, (down, mine, theirs, near), mate, work=two)
+    second, early = lax.optimization_barrier((second, early))
+    side = send(second, outer_to_inner)
+    late_out, pooled_out = call(
+        merge_kernel, "merge", [bare, pooled], (second, early, got, down, mine, theirs), halves=True
+    )
+    pooled_late = send(pooled_out, vertical_inner)
+    late = send(late_out, vertical_inner)
+    local = call(own_kernel, "own", bare32, (own_msg, mine, theirs, near), mate, work=two)
+    block_so_far, pooled_all = call(
+        blend_kernel,
+        "blend",
+        [bare32, pooled],
+        (local, side, got, down, mine, theirs, early, pooled_late),
+        halves=True,
+    )
+    sections = lax.axis_size("sec")
+    before = lax.ppermute(pooled_all, "sec", [(i, i + 1) for i in range(sections - 1)])
+    after = lax.ppermute(pooled_all, "sec", [(i + 1, i) for i in range(sections - 1)])
+    blended = call(last_kernel, "last", bare, (block_so_far, late), work=(1e6, 2e6))
+    index = lax.axis_index("sec")
+    present = 4.0 - (index == 0).astype(f32) - (index == sections - 1).astype(f32)
+    level = (before.astype(f32) + 2.0 * pooled_all.astype(f32) + after.astype(f32)) / present
+    return blended[None, None], level.astype(bf16)[None, None]
+
+
+def per_device(*args):
+    if lax.axis_size("blk") == 2 * GY:
+        return two_row_device(*args)
+    return general_device(*args)
+
+
 def solution(mesh):
     return jax.shard_map(
         per_device,

time: 69.7 us -> 55.2 us (0.79)
  the two profiles are of different devices: /device:TPU:28 before, /device:TPU:12 now
where the time goes in v2:
time: 55.2 us; the launch traced here: 54.9 us
  waiting for transfers between devices  20.2 us (37%)
  starting transfers between devices  18.9 us (34%)
  Pallas kernels  14.2 us (26%)
  other arithmetic  0.81 us (1%)
  between operations  0.76 us (1%)
    ppermute x8, waiting for transfers between devices, send(): return lax.ppermute(value, 'blk', pairs)  15.9 us
    ppermute x8, starting transfers between devices, send(): return lax.ppermute(value, 'blk', pairs)  13 us
    pallas_call x6, Pallas kernels, call(): pl.pallas_call(kernel, name=name, out_shape=out_shape, in_specs=[vmem()]...  11.6 us
    ppermute x1, waiting for transfers between devices, two_row_device(): lax.ppermute(pooled_all, 'sec', [(i, i + 1) for i in range(sections - 1)])  4.27 us
    ppermute x1, starting transfers between devices, two_row_device(): lax.ppermute(pooled_all, 'sec', [(i + 1, i) for i in range(sections - 1)])  3.36 us
    ppermute x1, starting transfers between devices, two_row_device(): lax.ppermute(pooled_all, 'sec', [(i, i + 1) for i in range(sections - 1)])  2.49 us
    pallas_call x1, Pallas kernels, fetch(): pl.pallas_call(fetch_kernel, name='fetch', out_shape=pltpu.VMEM(tile.shap...  1.57 us
  transfers between devices with their start and end apart: 10, of which 6 were waited for; matrix products, arithmetic and copies ran while one was open for 0% of the time, Pallas kernels for 21%

profile of v2, /device:TPU:12, one launch (start us, length us, event | category | flops | bytes accessed | tf_op | source)
XLA Modules:
  0.0 54.9 jit_solution(16724699353289599759)
XLA Ops:
  0.6 1.0 %prepare.1 = (bf16[32,512]{1,0:T(8,128)(2,1)S(1)}, bf16[32,512]{1,0:T(8,128)(2,1)S(1)}, bf16[32,512]{1,0:T(8,128)(2,1)S(1)}, bf16[32,512]{1,0:T(8,128)(2,1)S(1)}) custom-call(bf16[9,4,512]{2,1,0:T(4,128)(2,1)} %bitcast.17, bf16[9,4,512]{2,1,0:T(4,128)(2,1)} %bitcast.18, s32[9,1,512]{2,1,0:T(1,128)} %bitcast.19, s32[9,1,512]{2,1,0:T(1,128)} %bitcast.20, ...), custom_call_target="tpu_custom_call" | custom-call | flops 1000000 | bytes 200000 | tf_op jit(solution)/shard_map/prepare/pallas_call | solution.py:426
  1.6 0.1 collective-permute-start
  1.7 1.2 %collective-permute-done.theirs_ref = bf16[32,512]{1,0:T(8,128)(2,1)S(1)} collective-permute-done((bf16[32,512]{1,0:T(8,128)(2,1)S(1)}, bf16[32,512]{1,0:T(8,128)(2,1)S(1)}, u32[]{:S(2)}, u32[]{:S(2)}) %collective-permute-start) | collective-permute-done | bytes 32800 | tf_op jit(solution)/shard_map/ppermute | solution.py:653
  2.9 0.2 collective-permute-start.1
  3.1 0.1 broadcast_select_fusion.1
  3.1 1.6 %collective-permute-start.2 = (bf16[32,512]{1,0:T(8,128)(2,1)S(1)}, bf16[32,512]{1,0:T(8,128)(2,1)S(1)}, u32[]{:S(2)}, u32[]{:S(2)}) collective-permute-start(bf16[32,512]{1,0:T(8,128)(2,1)S(1)} %get-tuple-element.31), channel_id=1, source_target_pairs={{0,4},{3,7},{4,0},{7,3},{1,6},{2,5},{6,1},{5,2},{8,12},{11,15},{12... | collective-permute-start | bytes 98312 | tf_op jit(solution)/shard_map/ppermute | solution.py:653
  4.7 1.2 %collective-permute-start.3 = (bf16[32,512]{1,0:T(8,128)(2,1)S(1)}, bf16[32,512]{1,0:T(8,128)(2,1)S(1)}, u32[]{:S(2)}, u32[]{:S(2)}) collective-permute-start(bf16[32,512]{1,0:T(8,128)(2,1)S(1)} %get-tuple-element.30), channel_id=1, source_target_pairs={{0,3},{4,7},{3,0},{7,4},{1,5},{2,6},{5,1},{6,2},{8,11},{12,15},{11... | collective-permute-start | bytes 98312 | tf_op jit(solution)/shard_map/ppermute | solution.py:653
  6.0 1.6 %fetch.1.tile_ref = bf16[1024,1024]{1,0:T(8,128)(2,1)S(1)} custom-call(bf16[1024,1024]{1,0:T(8,128)(2,1)} %bitcast.15), custom_call_target="tpu_custom_call" | custom-call | flops 1000000 | bytes 4000000 | tf_op jit(solution)/shard_map/fetch/pallas_call | solution.py:454
  7.5 0.0 collective-permute-done.2.got_ref
  7.5 2.0 %collective-permute-done.3.down_ref = bf16[32,512]{1,0:T(8,128)(2,1)S(1)} collective-permute-done((bf16[32,512]{1,0:T(8,128)(2,1)S(1)}, bf16[32,512]{1,0:T(8,128)(2,1)S(1)}, u32[]{:S(2)}, u32[]{:S(2)}) %collective-permute-start.3) | collective-permute-done | bytes 32800 | tf_op jit(solution)/shard_map/ppermute | solution.py:653
  9.5 0.0 collective-permute-done.1.mate_ref
  9.5 1.7 %first.1 = bf16[528,512]{1,0:T(8,128)(2,1)S(1)} custom-call(bf16[32,512]{1,0:T(8,128)(2,1)S(1)} %collective-permute-done.2.got_ref, bf16[32,512]{1,0:T(8,128)(2,1)S(1)} %get-tuple-element.17.mine_ref, bf16[32,512]{1,0:T(8,128)(2,1)S(1)} %collective-permute-done.theirs_ref, bf16[1024,1024]{1,0:T(8,128)(2,1)S(1)} %fetch.1.tile_ref, ...), custom_call_target="tpu_custom_call" | custom-call | flops 4000000000 | bytes 4000000 | tf_op jit(solution)/shard_map/first/pallas_call | solution.py:633
  11.2 1.3 %collective-permute-start.4 = (bf16[528,512]{1,0:T(8,128)(2,1)S(1)}, bf16[528,512]{1,0:T(8,128)(2,1)S(1)}, u32[]{:S(2)}, u32[]{:S(2)}) collective-permute-start(bf16[528,512]{1,0:T(8,128)(2,1)S(1)} %first.1), channel_id=1, source_target_pairs={{0,4},{3,7},{4,0},{7,3},{1,2},{5,6},{2,1},{6,5},{8,12},{11,15},{12... | collective-permute-start | bytes 1622024 | tf_op jit(solution)/shard_map/ppermute | solution.py:653
  12.5 3.9 %second.1.local_ref = bf16[528,512]{1,0:T(8,128)(2,1)S(1)} custom-call(bf16[32,512]{1,0:T(8,128)(2,1)S(1)} %collective-permute-done.3.down_ref, bf16[32,512]{1,0:T(8,128)(2,1)S(1)} %get-tuple-element.17.mine_ref, bf16[32,512]{1,0:T(8,128)(2,1)S(1)} %collective-permute-done.theirs_ref, bf16[1024,1024]{1,0:T(8,128)(2,1)S(1)} %fetch.1.tile_ref, ...), custom_call_target="tpu_custom_call" | custom-call | flops 4000000000 | bytes 4000000 | tf_op jit(solution)/shard_map/second/pallas_call | solution.py:633
  16.4 6.9 %collective-permute-done.4.over_ref.early_ref = bf16[528,512]{1,0:T(8,128)(2,1)S(1)} collective-permute-done((bf16[528,512]{1,0:T(8,128)(2,1)S(1)}, bf16[528,512]{1,0:T(8,128)(2,1)S(1)}, u32[]{:S(2)}, u32[]{:S(2)}) %collective-permute-start.4) | collective-permute-done | bytes 540704 | tf_op jit(solution)/shard_map/ppermute | solution.py:653
  23.3 1.3 %collective-permute-start.5 = (bf16[528,512]{1,0:T(8,128)(2,1)S(1)}, bf16[528,512]{1,0:T(8,128)(2,1)S(1)}, u32[]{:S(2)}, u32[]{:S(2)}) collective-permute-start(bf16[528,512]{1,0:T(8,128)(2,1)S(1)} %second.1.local_ref), channel_id=1, source_target_pairs={{0,2},{3,1},{4,6},{7,5},{8,10},{11,9},{12,14},{15,13},{16,18},{19,... | collective-permute-start | bytes 1622024 | tf_op jit(solution)/shard_map/ppermute | solution.py:653
  24.6 0.6 %merge.1 = (bf16[512,512]{1,0:T(8,128)(2,1)S(1)}, bf16[256,256]{1,0:T(8,128)(2,1)S(1)}) custom-call(bf16[528,512]{1,0:T(8,128)(2,1)S(1)} %second.1.local_ref, bf16[528,512]{1,0:T(8,128)(2,1)S(1)} %collective-permute-done.4.over_ref.early_ref, bf16[32,512]{1,0:T(8,128)(2,1)S(1)} %collective-permute-done.2.got_ref, ...), custom_call_target="tpu_custom_call" | custom-call | flops 1000000000 | bytes 4000000 | tf_op jit(solution)/shard_map/merge/pallas_call | solution.py:633
  25.2 5.3 %collective-permute-start.6 = (bf16[256,256]{1,0:T(8,128)(2,1)S(1)}, bf16[256,256]{1,0:T(8,128)(2,1)S(1)}, u32[]{:S(2)}, u32[]{:S(2)}) collective-permute-start(bf16[256,256]{1,0:T(8,128)(2,1)S(1)} %get-tuple-element.26), channel_id=1, source_target_pairs={{1,5},{2,6},{5,1},{6,2},{9,13},{10,14},{13,9},{14,10},{17,21},{18,... | collective-permute-start | bytes 393224 | tf_op jit(solution)/shard_map/ppermute | solution.py:653
  30.5 2.1 %collective-permute-start.7 = (bf16[512,512]{1,0:T(8,128)(2,1)S(1)}, bf16[512,512]{1,0:T(8,128)(2,1)S(1)}, u32[]{:S(2)}, u32[]{:S(2)}) collective-permute-start(bf16[512,512]{1,0:T(8,128)(2,1)S(1)} %get-tuple-element.28), channel_id=1, source_target_pairs={{1,5},{2,6},{5,1},{6,2},{9,13},{10,14},{13,9},{14,10},{17,21},{18,... | collective-permute-start | bytes 1572872 | tf_op jit(solution)/shard_map/ppermute | solution.py:653
  32.6 4.0 %own.1.local_ref = f32[512,512]{1,0:T(8,128)S(1)} custom-call(bf16[32,512]{1,0:T(8,128)(2,1)S(1)} %get-tuple-element.16.own_ref, bf16[32,512]{1,0:T(8,128)(2,1)S(1)} %get-tuple-element.17.mine_ref, bf16[32,512]{1,0:T(8,128)(2,1)S(1)} %collective-permute-done.theirs_ref, bf16[1024,1024]{1,0:T(8,128)(2,1)S(1)} %fetch.1.tile_ref, ...), custom_call_target="tpu_custom_call" | custom-call | flops 4000000000 | bytes 4000000 | tf_op jit(solution)/shard_map/own/pallas_call | solution.py:633
  36.6 0.0 collective-permute-done.6.pooled_early_ref
  36.6 5.8 %collective-permute-done.5.side_ref = bf16[528,512]{1,0:T(8,128)(2,1)S(1)} collective-permute-done((bf16[528,512]{1,0:T(8,128)(2,1)S(1)}, bf16[528,512]{1,0:T(8,128)(2,1)S(1)}, u32[]{:S(2)}, u32[]{:S(2)}) %collective-permute-start.5) | collective-permute-done | bytes 540704 | tf_op jit(solution)/shard_map/ppermute | solution.py:653
  42.4 0.6 %blend.1 = (f32[512,512]{1,0:T(8,128)S(1)}, bf16[256,256]{1,0:T(8,128)(2,1)S(1)}) custom-call(f32[512,512]{1,0:T(8,128)S(1)} %own.1.local_ref, bf16[528,512]{1,0:T(8,128)(2,1)S(1)} %collective-permute-done.5.side_ref, bf16[32,512]{1,0:T(8,128)(2,1)S(1)} %collective-permute-done.2.got_ref, bf16[32,512]{1,0:T(8,128)(2,1)S(1)} %collective-permute-done.3.down_ref, ...), custom_call_target="tpu_custom_call" | custom-call | flops 1000000000 | bytes 4000000 | tf_op jit(solution)/shard_map/blend/pallas_call | solution.py:633
  43.0 3.4 %collective-permute-start.9 = (bf16[256,256]{1,0:T(8,128)(2,1)S(1)}, bf16[256,256]{1,0:T(8,128)(2,1)S(1)}, u32[]{:S(2)}, u32[]{:S(2)}) collective-permute-start(bf16[256,256]{1,0:T(8,128)(2,1)S(1)} %get-tuple-element.29), channel_id=1, source_target_pairs={{8,0},{16,8},{24,16},{9,1},{17,9},{25,17},{10,2},{18,10},{26,18},{... | collective-permute-start | bytes 393224 | tf_op jit(solution)/shard_map/ppermute | solution.py:714
  46.4 2.5 %collective-permute-start.8 = (bf16[256,256]{1,0:T(8,128)(2,1)S(1)}, bf16[256,256]{1,0:T(8,128)(2,1)S(1)}, u32[]{:S(2)}, u32[]{:S(2)}) collective-permute-start(bf16[256,256]{1,0:T(8,128)(2,1)S(1)} %get-tuple-element.29), channel_id=1, source_target_pairs={{0,8},{8,16},{16,24},{1,9},{9,17},{17,25},{2,10},{10,18},{18,26},{... | collective-permute-start | bytes 393224 | tf_op jit(solution)/shard_map/ppermute | solution.py:713
  48.9 0.0 collective-permute-done.7.late_ref
  48.9 0.9 %last.1 = bf16[512,512]{1,0:T(8,128)(2,1)} custom-call(f32[512,512]{1,0:T(8,128)S(1)} %get-tuple-element.27.block_ref, bf16[512,512]{1,0:T(8,128)(2,1)S(1)} %collective-permute-done.7.late_ref), custom_call_target="tpu_custom_call" | custom-call | flops 1000000 | bytes 2000000 | tf_op jit(solution)/shard_map/last/pallas_call | solution.py:633
  49.8 0.1 collective-permute-done.9
  49.9 4.3 %collective-permute-done.8 = bf16[256,256]{1,0:T(8,128)(2,1)S(1)} collective-permute-done((bf16[256,256]{1,0:T(8,128)(2,1)S(1)}, bf16[256,256]{1,0:T(8,128)(2,1)S(1)}, u32[]{:S(2)}, u32[]{:S(2)}) %collective-permute-start.8) | collective-permute-done | bytes 131104 | tf_op jit(solution)/shard_map/ppermute | solution.py:713
  54.1 0.7 %fusion = bf16[1,1,256,256]{3,2,1,0:T(8,128)(2,1)} fusion(f32[]{:T(128)S(6)} %sub.7, bf16[256,256]{1,0:T(8,128)(2,1)S(1)} %collective-permute-done.9, bf16[256,256]{1,0:T(8,128)(2,1)S(1)} %get-tuple-element.29, bf16[256,256]{1,0:T(8,128)(2,1)S(1)} %collective-permute-done.8), kind=kLoop, calls=%fused_computation.1 | loop fusion | flops 524288 | bytes 524292 | tf_op jit(solution)/shard_map/broadcast_in_dim | solution.py:719
  (1 shorter events, 0.0 us)
Async XLA Ops:
  1.6 1.3 %collective-permute-start = (bf16[32,512]{1,0:T(8,128)(2,1)S(1)}, bf16[32,512]{1,0:T(8,128)(2,1)S(1)}, u32[]{:S(2)}, u32[]{:S(2)}) collective-permute-start(bf16[32,512]{1,0:T(8,128)(2,1)S(1)} %get-tuple-element.18), channel_id=1, source_target_pairs={{0,1},{1,0},{2,3},{3,2},{4,5},{5,4},{6,7},{7,6},{8,9},{9,8},{10,11... | collective-permute-start | bytes 98312 | tf_op jit(solution)/shard_map/ppermute | solution.py:653
  2.9 6.7 %collective-permute-start.1 = (bf16[1024,1024]{1,0:T(8,128)(2,1)}, bf16[1024,1024]{1,0:T(8,128)(2,1)}, u32[]{:S(2)}, u32[]{:S(2)}) collective-permute-start(bf16[1024,1024]{1,0:T(8,128)(2,1)} %bitcast.14), channel_id=1, source_target_pairs={{0,1},{1,0},{2,3},{3,2},{4,5},{5,4},{6,7},{7,6},{8,9},{9,8},{10,11... | collective-permute-start | bytes 6291464 | tf_op jit(solution)/shard_map/ppermute | solution.py:653
  3.1 4.4 %collective-permute-start.2 = (bf16[32,512]{1,0:T(8,128)(2,1)S(1)}, bf16[32,512]{1,0:T(8,128)(2,1)S(1)}, u32[]{:S(2)}, u32[]{:S(2)}) collective-permute-start(bf16[32,512]{1,0:T(8,128)(2,1)S(1)} %get-tuple-element.31), channel_id=1, source_target_pairs={{0,4},{3,7},{4,0},{7,3},{1,6},{2,5},{6,1},{5,2},{8,12},{11,15},{12... | collective-permute-start | bytes 98312 | tf_op jit(solution)/shard_map/ppermute | solution.py:653
  4.7 4.8 %collective-permute-start.3 = (bf16[32,512]{1,0:T(8,128)(2,1)S(1)}, bf16[32,512]{1,0:T(8,128)(2,1)S(1)}, u32[]{:S(2)}, u32[]{:S(2)}) collective-permute-start(bf16[32,512]{1,0:T(8,128)(2,1)S(1)} %get-tuple-element.30), channel_id=1, source_target_pairs={{0,3},{4,7},{3,0},{7,4},{1,5},{2,6},{5,1},{6,2},{8,11},{12,15},{11... | collective-permute-start | bytes 98312 | tf_op jit(solution)/shard_map/ppermute | solution.py:653
  11.2 12.1 %collective-permute-start.4 = (bf16[528,512]{1,0:T(8,128)(2,1)S(1)}, bf16[528,512]{1,0:T(8,128)(2,1)S(1)}, u32[]{:S(2)}, u32[]{:S(2)}) collective-permute-start(bf16[528,512]{1,0:T(8,128)(2,1)S(1)} %first.1), channel_id=1, source_target_pairs={{0,4},{3,7},{4,0},{7,3},{1,2},{5,6},{2,1},{6,5},{8,12},{11,15},{12... | collective-permute-start | bytes 1622024 | tf_op jit(solution)/shard_map/ppermute | solution.py:653
  23.3 19.1 %collective-permute-start.5 = (bf16[528,512]{1,0:T(8,128)(2,1)S(1)}, bf16[528,512]{1,0:T(8,128)(2,1)S(1)}, u32[]{:S(2)}, u32[]{:S(2)}) collective-permute-start(bf16[528,512]{1,0:T(8,128)(2,1)S(1)} %second.1.local_ref), channel_id=1, source_target_pairs={{0,2},{3,1},{4,6},{7,5},{8,10},{11,9},{12,14},{15,13},{16,18},{19,... | collective-permute-start | bytes 1622024 | tf_op jit(solution)/shard_map/ppermute | solution.py:653
  25.2 11.4 %collective-permute-start.6 = (bf16[256,256]{1,0:T(8,128)(2,1)S(1)}, bf16[256,256]{1,0:T(8,128)(2,1)S(1)}, u32[]{:S(2)}, u32[]{:S(2)}) collective-permute-start(bf16[256,256]{1,0:T(8,128)(2,1)S(1)} %get-tuple-element.26), channel_id=1, source_target_pairs={{1,5},{2,6},{5,1},{6,2},{9,13},{10,14},{13,9},{14,10},{17,21},{18,... | collective-permute-start | bytes 393224 | tf_op jit(solution)/shard_map/ppermute | solution.py:653
  30.5 18.4 %collective-permute-start.7 = (bf16[512,512]{1,0:T(8,128)(2,1)S(1)}, bf16[512,512]{1,0:T(8,128)(2,1)S(1)}, u32[]{:S(2)}, u32[]{:S(2)}) collective-permute-start(bf16[512,512]{1,0:T(8,128)(2,1)S(1)} %get-tuple-element.28), channel_id=1, source_target_pairs={{1,5},{2,6},{5,1},{6,2},{9,13},{10,14},{13,9},{14,10},{17,21},{18,... | collective-permute-start | bytes 1572872 | tf_op jit(solution)/shard_map/ppermute | solution.py:653
  43.0 6.9 %collective-permute-start.9 = (bf16[256,256]{1,0:T(8,128)(2,1)S(1)}, bf16[256,256]{1,0:T(8,128)(2,1)S(1)}, u32[]{:S(2)}, u32[]{:S(2)}) collective-permute-start(bf16[256,256]{1,0:T(8,128)(2,1)S(1)} %get-tuple-element.29), channel_id=1, source_target_pairs={{8,0},{16,8},{24,16},{9,1},{17,9},{25,17},{10,2},{18,10},{26,18},{... | collective-permute-start | bytes 393224 | tf_op jit(solution)/shard_map/ppermute | solution.py:714
  46.4 7.8 %collective-permute-start.8 = (bf16[256,256]{1,0:T(8,128)(2,1)S(1)}, bf16[256,256]{1,0:T(8,128)(2,1)S(1)}, u32[]{:S(2)}, u32[]{:S(2)}) collective-permute-start(bf16[256,256]{1,0:T(8,128)(2,1)S(1)} %get-tuple-element.29), channel_id=1, source_target_pairs={{0,8},{8,16},{16,24},{1,9},{9,17},{17,25},{2,10},{10,18},{18,26},{... | collective-permute-start | bytes 393224 | tf_op jit(solution)/shard_map/ppermute | solution.py:713

commit v3 on v2

--- a/solution.py
+++ b/solution.py
@@ -689,19 +689,22 @@
     bare32 = jax.ShapeDtypeStruct((edge, edge), f32)
     pooled = jax.ShapeDtypeStruct((edge // 2, edge // 2), bf16)
     two = (4e9, 4e6)
-
-    got, down = lax.optimization_barrier((got, down))
-    first = call(first_kernel, "first", block, (got, mine, theirs, near), mate, work=two)
+    tiny = (1e4, 1e4)
+
+    first = call(first_kernel, "first", block, (got, mine, theirs, near), mate, work=tiny)
     early = send(first, vertical_outer + across_inner)
+    down, first = lax.optimization_barrier((down, first))
     second = call(second_kernel, "second", block, (down, mine, theirs, near), mate, work=two)
-    second, early = lax.optimization_barrier((second, early))
+    own_msg, second = lax.optimization_barrier((own_msg, second))
+    local = call(own_kernel, "own", bare32, (own_msg, mine, theirs, near), mate, work=two)
+    second, local = lax.optimization_barrier((second, local))
     side = send(second, outer_to_inner)
+    early, local = lax.optimization_barrier((early, local))
     late_out, pooled_out = call(
         merge_kernel, "merge", [bare, pooled], (second, early, got, down, mine, theirs), halves=True
     )
     pooled_late = send(pooled_out, vertical_inner)
     late = send(late_out, vertical_inner)
-    local = call(own_kernel, "own", bare32, (own_msg, mine, theirs, near), mate, work=two)
     block_so_far, pooled_all = call(
         blend_kernel,
         "blend",

time: 55.2 us -> 48.1 us (0.87)
  the two profiles are of different devices: /device:TPU:12 before, /device:TPU:28 now
where the time goes in v3:
time: 48.1 us; the launch traced here: 47.9 us
  starting transfers between devices  16.4 us (34%)
  waiting for transfers between devices  15.6 us (32%)
  Pallas kernels  14.4 us (30%)
  other arithmetic  0.81 us (2%)
  between operations  0.74 us (2%)
    pallas_call x6, Pallas kernels, call(): pl.pallas_call(kernel, name=name, out_shape=out_shape, in_specs=[vmem()]...  11.8 us
    ppermute x8, starting transfers between devices, send(): return lax.ppermute(value, 'blk', pairs)  10.5 us
    ppermute x8, waiting for transfers between devices, send(): return lax.ppermute(value, 'blk', pairs)  10.4 us
    ppermute x1, waiting for transfers between devices, two_row_device(): lax.ppermute(pooled_all, 'sec', [(i, i + 1) for i in range(sections - 1)])  4.22 us
    ppermute x1, starting transfers between devices, two_row_device(): lax.ppermute(pooled_all, 'sec', [(i + 1, i) for i in range(sections - 1)])  3.31 us
    ppermute x1, starting transfers between devices, two_row_device(): lax.ppermute(pooled_all, 'sec', [(i, i + 1) for i in range(sections - 1)])  2.53 us
    pallas_call x1, Pallas kernels, fetch(): pl.pallas_call(fetch_kernel, name='fetch', out_shape=pltpu.VMEM(tile.shap...  1.57 us
    ppermute x1, waiting for transfers between devices, two_row_device(): lax.ppermute(pooled_all, 'sec', [(i + 1, i) for i in range(sections - 1)])  0.99 us
  transfers between devices with their start and end apart: 10, of which 6 were waited for; matrix products, arithmetic and copies ran while one was open for 2% of the time, Pallas kernels for 26%

profile of v3, /device:TPU:28, one launch (start us, length us, event | category | flops | bytes accessed | tf_op | source)
XLA Modules:
  0.0 47.9 jit_solution(10249053892745144000)
XLA Ops:
  0.6 1.0 %prepare.1 = (bf16[32,512]{1,0:T(8,128)(2,1)S(1)}, bf16[32,512]{1,0:T(8,128)(2,1)S(1)}, bf16[32,512]{1,0:T(8,128)(2,1)S(1)}, bf16[32,512]{1,0:T(8,128)(2,1)S(1)}) custom-call(bf16[9,4,512]{2,1,0:T(4,128)(2,1)} %bitcast.17, bf16[9,4,512]{2,1,0:T(4,128)(2,1)} %bitcast.18, s32[9,1,512]{2,1,0:T(1,128)} %bitcast.19, s32[9,1,512]{2,1,0:T(1,128)} %bitcast.20, ...), custom_call_target="tpu_custom_call" | custom-call | flops 1000000 | bytes 200000 | tf_op jit(solution)/shard_map/prepare/pallas_call | solution.py:426
  1.6 0.1 collective-permute-start
  1.7 1.2 %collective-permute-done.theirs_ref = bf16[32,512]{1,0:T(8,128)(2,1)S(1)} collective-permute-done((bf16[32,512]{1,0:T(8,128)(2,1)S(1)}, bf16[32,512]{1,0:T(8,128)(2,1)S(1)}, u32[]{:S(2)}, u32[]{:S(2)}) %collective-permute-start) | collective-permute-done | bytes 32800 | tf_op jit(solution)/shard_map/ppermute | solution.py:653
  2.9 0.2 collective-permute-start.2
  3.1 0.1 broadcast_select_fusion.1
  3.1 0.2 collective-permute-start.1
  3.4 1.7 %collective-permute-start.4 = (bf16[32,512]{1,0:T(8,128)(2,1)S(1)}, bf16[32,512]{1,0:T(8,128)(2,1)S(1)}, u32[]{:S(2)}, u32[]{:S(2)}) collective-permute-start(bf16[32,512]{1,0:T(8,128)(2,1)S(1)} %get-tuple-element.36), channel_id=1, source_target_pairs={{0,3},{4,7},{3,0},{7,4},{1,5},{2,6},{5,1},{6,2},{8,11},{12,15},{11... | collective-permute-start | bytes 98312 | tf_op jit(solution)/shard_map/ppermute | solution.py:653
  5.1 1.6 %fetch.1.tile_ref = bf16[1024,1024]{1,0:T(8,128)(2,1)S(1)} custom-call(bf16[1024,1024]{1,0:T(8,128)(2,1)} %bitcast.15), custom_call_target="tpu_custom_call" | custom-call | flops 1000000 | bytes 4000000 | tf_op jit(solution)/shard_map/fetch/pallas_call | solution.py:454
  6.6 1.7 %collective-permute-done.1.got_ref = bf16[32,512]{1,0:T(8,128)(2,1)S(1)} collective-permute-done((bf16[32,512]{1,0:T(8,128)(2,1)S(1)}, bf16[32,512]{1,0:T(8,128)(2,1)S(1)}, u32[]{:S(2)}, u32[]{:S(2)}) %collective-permute-start.1) | collective-permute-done | bytes 32800 | tf_op jit(solution)/shard_map/ppermute | solution.py:653
  8.3 0.0 collective-permute-done.2.mate_ref
  8.3 1.7 %first.1 = bf16[528,512]{1,0:T(8,128)(2,1)S(1)} custom-call(bf16[32,512]{1,0:T(8,128)(2,1)S(1)} %collective-permute-done.1.got_ref, bf16[32,512]{1,0:T(8,128)(2,1)S(1)} %get-tuple-element.21.mine_ref, bf16[32,512]{1,0:T(8,128)(2,1)S(1)} %collective-permute-done.theirs_ref, bf16[1024,1024]{1,0:T(8,128)(2,1)S(1)} %fetch.1.tile_ref, ...), custom_call_target="tpu_custom_call" | custom-call | flops 10000 | bytes 10000 | tf_op jit(solution)/shard_map/first/pallas_call | solution.py:633
  10.0 0.3 collective-permute-start.3
  10.4 0.0 collective-permute-done.4.down_ref
  10.4 4.1 %second.1.local_ref = bf16[528,512]{1,0:T(8,128)(2,1)S(1)} custom-call(bf16[32,512]{1,0:T(8,128)(2,1)S(1)} %collective-permute-done.4.down_ref, bf16[32,512]{1,0:T(8,128)(2,1)S(1)} %get-tuple-element.21.mine_ref, bf16[32,512]{1,0:T(8,128)(2,1)S(1)} %collective-permute-done.theirs_ref, bf16[1024,1024]{1,0:T(8,128)(2,1)S(1)} %fetch.1.tile_ref, ...), custom_call_target="tpu_custom_call" | custom-call | flops 4000000000 | bytes 4000000 | tf_op jit(solution)/shard_map/second/pallas_call | solution.py:633
  14.5 4.0 %own.1.local_ref = f32[512,512]{1,0:T(8,128)S(1)} custom-call(bf16[32,512]{1,0:T(8,128)(2,1)S(1)} %get-tuple-element.27.own_ref, bf16[32,512]{1,0:T(8,128)(2,1)S(1)} %get-tuple-element.21.mine_ref, bf16[32,512]{1,0:T(8,128)(2,1)S(1)} %collective-permute-done.theirs_ref, bf16[1024,1024]{1,0:T(8,128)(2,1)S(1)} %fetch.1.tile_ref, ...), custom_call_target="tpu_custom_call" | custom-call | flops 4000000000 | bytes 4000000 | tf_op jit(solution)/shard_map/own/pallas_call | solution.py:633
  18.4 1.3 %collective-permute-start.5 = (bf16[528,512]{1,0:T(8,128)(2,1)S(1)}, bf16[528,512]{1,0:T(8,128)(2,1)S(1)}, u32[]{:S(2)}, u32[]{:S(2)}) collective-permute-start(bf16[528,512]{1,0:T(8,128)(2,1)S(1)} %second.1.local_ref), channel_id=1, source_target_pairs={{0,2},{3,1},{4,6},{7,5},{8,10},{11,9},{12,14},{15,13},{16,18},{19,... | collective-permute-start | bytes 1622024 | tf_op jit(solution)/shard_map/ppermute | solution.py:653
  19.7 2.2 %collective-permute-done.3.over_ref.early_ref = bf16[528,512]{1,0:T(8,128)(2,1)S(1)} collective-permute-done((bf16[528,512]{1,0:T(8,128)(2,1)S(1)}, bf16[528,512]{1,0:T(8,128)(2,1)S(1)}, u32[]{:S(2)}, u32[]{:S(2)}) %collective-permute-start.3) | collective-permute-done | bytes 540704 | tf_op jit(solution)/shard_map/ppermute | solution.py:653
  21.9 0.6 %merge.1 = (bf16[512,512]{1,0:T(8,128)(2,1)S(1)}, bf16[256,256]{1,0:T(8,128)(2,1)S(1)}) custom-call(bf16[528,512]{1,0:T(8,128)(2,1)S(1)} %second.1.local_ref, bf16[528,512]{1,0:T(8,128)(2,1)S(1)} %collective-permute-done.3.over_ref.early_ref, bf16[32,512]{1,0:T(8,128)(2,1)S(1)} %collective-permute-done.1.got_ref, ...), custom_call_target="tpu_custom_call" | custom-call | flops 1000000000 | bytes 4000000 | tf_op jit(solution)/shard_map/merge/pallas_call | solution.py:633
  22.5 1.9 %collective-permute-start.6 = (bf16[256,256]{1,0:T(8,128)(2,1)S(1)}, bf16[256,256]{1,0:T(8,128)(2,1)S(1)}, u32[]{:S(2)}, u32[]{:S(2)}) collective-permute-start(bf16[256,256]{1,0:T(8,128)(2,1)S(1)} %get-tuple-element.32), channel_id=1, source_target_pairs={{1,5},{2,6},{5,1},{6,2},{9,13},{10,14},{13,9},{14,10},{17,21},{18,... | collective-permute-start | bytes 393224 | tf_op jit(solution)/shard_map/ppermute | solution.py:653
  24.4 4.8 %collective-permute-start.7 = (bf16[512,512]{1,0:T(8,128)(2,1)S(1)}, bf16[512,512]{1,0:T(8,128)(2,1)S(1)}, u32[]{:S(2)}, u32[]{:S(2)}) collective-permute-start(bf16[512,512]{1,0:T(8,128)(2,1)S(1)} %get-tuple-element.34), channel_id=1, source_target_pairs={{1,5},{2,6},{5,1},{6,2},{9,13},{10,14},{13,9},{14,10},{17,21},{18,... | collective-permute-start | bytes 1572872 | tf_op jit(solution)/shard_map/ppermute | solution.py:653
  29.2 5.3 %collective-permute-done.5.side_ref = bf16[528,512]{1,0:T(8,128)(2,1)S(1)} collective-permute-done((bf16[528,512]{1,0:T(8,128)(2,1)S(1)}, bf16[528,512]{1,0:T(8,128)(2,1)S(1)}, u32[]{:S(2)}, u32[]{:S(2)}) %collective-permute-start.5) | collective-permute-done | bytes 540704 | tf_op jit(solution)/shard_map/ppermute | solution.py:653
  34.6 0.0 collective-permute-done.6.pooled_early_ref
  34.6 0.6 %blend.1 = (f32[512,512]{1,0:T(8,128)S(1)}, bf16[256,256]{1,0:T(8,128)(2,1)S(1)}) custom-call(f32[512,512]{1,0:T(8,128)S(1)} %own.1.local_ref, bf16[528,512]{1,0:T(8,128)(2,1)S(1)} %collective-permute-done.5.side_ref, bf16[32,512]{1,0:T(8,128)(2,1)S(1)} %collective-permute-done.1.got_ref, bf16[32,512]{1,0:T(8,128)(2,1)S(1)} %collective-permute-done.4.down_ref, ...), custom_call_target="tpu_custom_call" | custom-call | flops 1000000000 | bytes 4000000 | tf_op jit(solution)/shard_map/blend/pallas_call | solution.py:633
  35.2 3.3 %collective-permute-start.9 = (bf16[256,256]{1,0:T(8,128)(2,1)S(1)}, bf16[256,256]{1,0:T(8,128)(2,1)S(1)}, u32[]{:S(2)}, u32[]{:S(2)}) collective-permute-start(bf16[256,256]{1,0:T(8,128)(2,1)S(1)} %get-tuple-element.35), channel_id=1, source_target_pairs={{8,0},{16,8},{24,16},{9,1},{17,9},{25,17},{10,2},{18,10},{26,18},{... | collective-permute-start | bytes 393224 | tf_op jit(solution)/shard_map/ppermute | solution.py:717
  38.5 2.5 %collective-permute-start.8 = (bf16[256,256]{1,0:T(8,128)(2,1)S(1)}, bf16[256,256]{1,0:T(8,128)(2,1)S(1)}, u32[]{:S(2)}, u32[]{:S(2)}) collective-permute-start(bf16[256,256]{1,0:T(8,128)(2,1)S(1)} %get-tuple-element.35), channel_id=1, source_target_pairs={{0,8},{8,16},{16,24},{1,9},{9,17},{17,25},{2,10},{10,18},{18,26},{... | collective-permute-start | bytes 393224 | tf_op jit(solution)/shard_map/ppermute | solution.py:716
  41.1 1.0 %collective-permute-done.9 = bf16[256,256]{1,0:T(8,128)(2,1)S(1)} collective-permute-done((bf16[256,256]{1,0:T(8,128)(2,1)S(1)}, bf16[256,256]{1,0:T(8,128)(2,1)S(1)}, u32[]{:S(2)}, u32[]{:S(2)}) %collective-permute-start.9) | collective-permute-done | bytes 131104 | tf_op jit(solution)/shard_map/ppermute | solution.py:717
  42.0 4.2 %collective-permute-done.8 = bf16[256,256]{1,0:T(8,128)(2,1)S(1)} collective-permute-done((bf16[256,256]{1,0:T(8,128)(2,1)S(1)}, bf16[256,256]{1,0:T(8,128)(2,1)S(1)}, u32[]{:S(2)}, u32[]{:S(2)}) %collective-permute-start.8) | collective-permute-done | bytes 131104 | tf_op jit(solution)/shard_map/ppermute | solution.py:716
  46.3 0.7 %fusion = bf16[1,1,256,256]{3,2,1,0:T(8,128)(2,1)} fusion(f32[]{:T(128)S(6)} %sub.7, bf16[256,256]{1,0:T(8,128)(2,1)S(1)} %collective-permute-done.9, bf16[256,256]{1,0:T(8,128)(2,1)S(1)} %get-tuple-element.35, bf16[256,256]{1,0:T(8,128)(2,1)S(1)} %collective-permute-done.8), kind=kLoop, calls=%fused_computation.1 | loop fusion | flops 524288 | bytes 524292 | tf_op jit(solution)/shard_map/broadcast_in_dim | solution.py:722
  47.0 0.0 collective-permute-done.7.late_ref
  47.0 0.9 %last.1 = bf16[512,512]{1,0:T(8,128)(2,1)} custom-call(f32[512,512]{1,0:T(8,128)S(1)} %get-tuple-element.33.block_ref, bf16[512,512]{1,0:T(8,128)(2,1)S(1)} %collective-permute-done.7.late_ref), custom_call_target="tpu_custom_call" | custom-call | flops 1000000 | bytes 2000000 | tf_op jit(solution)/shard_map/last/pallas_call | solution.py:633
  (1 shorter events, 0.0 us)
Async XLA Ops:
  1.6 1.3 %collective-permute-start = (bf16[32,512]{1,0:T(8,128)(2,1)S(1)}, bf16[32,512]{1,0:T(8,128)(2,1)S(1)}, u32[]{:S(2)}, u32[]{:S(2)}) collective-permute-start(bf16[32,512]{1,0:T(8,128)(2,1)S(1)} %get-tuple-element.19), channel_id=1, source_target_pairs={{0,1},{1,0},{2,3},{3,2},{4,5},{5,4},{6,7},{7,6},{8,9},{9,8},{10,11... | collective-permute-start | bytes 98312 | tf_op jit(solution)/shard_map/ppermute | solution.py:653
  2.9 5.4 %collective-permute-start.2 = (bf16[1024,1024]{1,0:T(8,128)(2,1)}, bf16[1024,1024]{1,0:T(8,128)(2,1)}, u32[]{:S(2)}, u32[]{:S(2)}) collective-permute-start(bf16[1024,1024]{1,0:T(8,128)(2,1)} %bitcast.14), channel_id=1, source_target_pairs={{0,1},{1,0},{2,3},{3,2},{4,5},{5,4},{6,7},{7,6},{8,9},{9,8},{10,11... | collective-permute-start | bytes 6291464 | tf_op jit(solution)/shard_map/ppermute | solution.py:653
  3.1 5.2 %collective-permute-start.1 = (bf16[32,512]{1,0:T(8,128)(2,1)S(1)}, bf16[32,512]{1,0:T(8,128)(2,1)S(1)}, u32[]{:S(2)}, u32[]{:S(2)}) collective-permute-start(bf16[32,512]{1,0:T(8,128)(2,1)S(1)} %get-tuple-element.37), channel_id=1, source_target_pairs={{0,4},{3,7},{4,0},{7,3},{1,6},{2,5},{6,1},{5,2},{8,12},{11,15},{12... | collective-permute-start | bytes 98312 | tf_op jit(solution)/shard_map/ppermute | solution.py:653
  3.4 7.0 %collective-permute-start.4 = (bf16[32,512]{1,0:T(8,128)(2,1)S(1)}, bf16[32,512]{1,0:T(8,128)(2,1)S(1)}, u32[]{:S(2)}, u32[]{:S(2)}) collective-permute-start(bf16[32,512]{1,0:T(8,128)(2,1)S(1)} %get-tuple-element.36), channel_id=1, source_target_pairs={{0,3},{4,7},{3,0},{7,4},{1,5},{2,6},{5,1},{6,2},{8,11},{12,15},{11... | collective-permute-start | bytes 98312 | tf_op jit(solution)/shard_map/ppermute | solution.py:653
  10.0 11.9 %collective-permute-start.3 = (bf16[528,512]{1,0:T(8,128)(2,1)S(1)}, bf16[528,512]{1,0:T(8,128)(2,1)S(1)}, u32[]{:S(2)}, u32[]{:S(2)}) collective-permute-start(bf16[528,512]{1,0:T(8,128)(2,1)S(1)} %first.1), channel_id=1, source_target_pairs={{0,4},{3,7},{4,0},{7,3},{1,2},{5,6},{2,1},{6,5},{8,12},{11,15},{12... | collective-permute-start | bytes 1622024 | tf_op jit(solution)/shard_map/ppermute | solution.py:653
  18.4 16.1 %collective-permute-start.5 = (bf16[528,512]{1,0:T(8,128)(2,1)S(1)}, bf16[528,512]{1,0:T(8,128)(2,1)S(1)}, u32[]{:S(2)}, u32[]{:S(2)}) collective-permute-start(bf16[528,512]{1,0:T(8,128)(2,1)S(1)} %second.1.local_ref), channel_id=1, source_target_pairs={{0,2},{3,1},{4,6},{7,5},{8,10},{11,9},{12,14},{15,13},{16,18},{19,... | collective-permute-start | bytes 1622024 | tf_op jit(solution)/shard_map/ppermute | solution.py:653
  22.5 12.1 %collective-permute-start.6 = (bf16[256,256]{1,0:T(8,128)(2,1)S(1)}, bf16[256,256]{1,0:T(8,128)(2,1)S(1)}, u32[]{:S(2)}, u32[]{:S(2)}) collective-permute-start(bf16[256,256]{1,0:T(8,128)(2,1)S(1)} %get-tuple-element.32), channel_id=1, source_target_pairs={{1,5},{2,6},{5,1},{6,2},{9,13},{10,14},{13,9},{14,10},{17,21},{18,... | collective-permute-start | bytes 393224 | tf_op jit(solution)/shard_map/ppermute | solution.py:653
  24.4 22.6 %collective-permute-start.7 = (bf16[512,512]{1,0:T(8,128)(2,1)S(1)}, bf16[512,512]{1,0:T(8,128)(2,1)S(1)}, u32[]{:S(2)}, u32[]{:S(2)}) collective-permute-start(bf16[512,512]{1,0:T(8,128)(2,1)S(1)} %get-tuple-element.34), channel_id=1, source_target_pairs={{1,5},{2,6},{5,1},{6,2},{9,13},{10,14},{13,9},{14,10},{17,21},{18,... | collective-permute-start | bytes 1572872 | tf_op jit(solution)/shard_map/ppermute | solution.py:653
  35.2 6.9 %collective-permute-start.9 = (bf16[256,256]{1,0:T(8,128)(2,1)S(1)}, bf16[256,256]{1,0:T(8,128)(2,1)S(1)}, u32[]{:S(2)}, u32[]{:S(2)}) collective-permute-start(bf16[256,256]{1,0:T(8,128)(2,1)S(1)} %get-tuple-element.35), channel_id=1, source_target_pairs={{8,0},{16,8},{24,16},{9,1},{17,9},{25,17},{10,2},{18,10},{26,18},{... | collective-permute-start | bytes 393224 | tf_op jit(solution)/shard_map/ppermute | solution.py:717
  38.5 7.8 %collective-permute-start.8 = (bf16[256,256]{1,0:T(8,128)(2,1)S(1)}, bf16[256,256]{1,0:T(8,128)(2,1)S(1)}, u32[]{:S(2)}, u32[]{:S(2)}) collective-permute-start(bf16[256,256]{1,0:T(8,128)(2,1)S(1)} %get-tuple-element.35), channel_id=1, source_target_pairs={{0,8},{8,16},{16,24},{1,9},{9,17},{17,25},{2,10},{10,18},{18,26},{... | collective-permute-start | bytes 393224 | tf_op jit(solution)/shard_map/ppermute | solution.py:716

commit v4 on v3

--- a/solution.py
+++ b/solution.py
@@ -351,6 +351,7 @@
 SCALARS = 28
 CORNER = 8
 ROWS = 32
+STRIPS = 8
 TILE = 1024
 PREPARE_VMEM = 40 * 1024 * 1024
 WORK_VMEM = 40 * 1024 * 1024
@@ -361,9 +362,9 @@
     return jnp.logical_or(column == 0, column == GY - 1)
 
 
-def prepare_kernel(rt_hbm, ct_hbm, rs_hbm, cs_hbm, foot_hbm, off_hbm, fr_hbm, fc_hbm, *refs):
-    outs = refs[:4]
-    rt_ref, ct_ref, rs_ref, cs_ref, fr_ref, fc_ref, foot_ref, off_ref, buf, sems = refs[4:]
+def prepare_kernel(rt_hbm, ct_hbm, rs_hbm, cs_hbm, foot_hbm, off_hbm, fr_hbm, fc_hbm, tile_hbm, *refs):
+    outs, near_ref = refs[:4], refs[4]
+    rt_ref, ct_ref, rs_ref, cs_ref, fr_ref, fc_ref, foot_ref, off_ref, buf, sems, tile_sems = refs[5:]
     pairs = [
         (off_hbm, off_ref),
         (foot_hbm, foot_ref),
@@ -376,6 +377,13 @@
     ]
     copies = [pltpu.make_async_copy(a, b, sems.at[i]) for i, (a, b) in enumerate(pairs)]
     for copy in copies:
+        copy.start()
+    strip = near_ref.shape[0] // STRIPS
+    strips = []
+    for n in range(STRIPS):
+        rows = pl.ds(n * strip, strip)
+        strips.append(pltpu.make_async_copy(tile_hbm.at[rows], near_ref.at[rows], tile_sems.at[n]))
+    for copy in strips:
         copy.start()
     for copy in copies:
         copy.wait()
@@ -391,11 +399,13 @@
         used = jnp.where(inside, foot_ref[0, jnp.clip(slot, 0, 8)], 0).astype(f32)
         scalars = jnp.where(lane == n, used, scalars)
 
+    outer = is_outer()
+
     def message(out_ref, slots, profile_row):
         row = scalars
         buf[...] = jnp.zeros(buf.shape, f32)
-        for half, (role, step) in enumerate(slots):
-            k = jnp.clip(slot_of(column, role, step), 0, 8)
+        for half, slot in enumerate(slots):
+            k = jnp.clip(slot, 0, 8)
             used = foot_ref[0, k].astype(f32)
             at = half * HALF
             buf[at : at + TAPS] = rt_ref[k].astype(f32)
@@ -414,53 +424,30 @@
         buf[SCALARS : SCALARS + 1] = row
         out_ref[...] = buf[...].astype(bf16)
 
-    message(outs[0], [(0, over), (1, over)], PROFILE)
-    message(outs[1], [(2, over)], PROFILE)
-    message(outs[2], [(2, 0)], BESIDE)
-    message(outs[3], [(0, 0), (1, 0)], PROFILE)
-
-
-def prepare(rt, ct, rs, cs, foot, off, fr, fc):
+    center, beside, across = (slot_of(column, role, over) for role in range(3))
+    message(outs[0], [jnp.where(outer, center, across), beside], PROFILE)
+    message(outs[1], [center, beside], PROFILE)
+    message(outs[2], [slot_of(column, 2, 0)], BESIDE)
+    message(outs[3], [slot_of(column, 0, 0), slot_of(column, 1, 0)], PROFILE)
+    for copy in strips:
+        copy.wait()
+
+
+def prepare(rt, ct, rs, cs, foot, off, fr, fc, tile):
     edge = fr.shape[1]
-    args = [pltpu.with_memory_space_constraint(x, pltpu.HBM) for x in (rt, ct, rs, cs, foot, off, fr, fc)]
+    args = [pltpu.with_memory_space_constraint(x, pltpu.HBM) for x in (rt, ct, rs, cs, foot, off, fr, fc, tile)]
     return pl.pallas_call(
         prepare_kernel,
         name="prepare",
-        out_shape=[jax.ShapeDtypeStruct((ROWS, edge), bf16)] * 4,
-        in_specs=[hbm()] * 8,
-        out_specs=[vmem()] * 4,
+        out_shape=[jax.ShapeDtypeStruct((ROWS, edge), bf16)] * 4 + [jax.ShapeDtypeStruct(tile.shape, bf16)],
+        in_specs=[hbm()] * 9,
+        out_specs=[vmem()] * 5,
         scratch_shapes=[pltpu.VMEM(x.shape, x.dtype) for x in (rt, ct, rs, cs, fr, fc)]
         + [pltpu.SMEM(x.shape, x.dtype) for x in (foot, off)]
-        + [pltpu.VMEM((ROWS, edge), f32), pltpu.SemaphoreType.DMA((8,))],
+        + [pltpu.VMEM((ROWS, edge), f32), pltpu.SemaphoreType.DMA((8,)), pltpu.SemaphoreType.DMA((STRIPS,))],
         compiler_params=pltpu.CompilerParams(vmem_limit_bytes=PREPARE_VMEM),
         cost_estimate=cost(1e6, 2e5),
     )(*args)
-
-
-def fetch_kernel(tile_ref, out_ref, sems):
-    parts = sems.shape[0]
-    size = out_ref.shape[0] // parts
-    copies = [
-        pltpu.make_async_copy(tile_ref.at[pl.ds(n * size, size)], out_ref.at[pl.ds(n * size, size)], sems.at[n])
-        for n in range(parts)
-    ]
-    for copy in copies:
-        copy.start()
-    for copy in copies:
-        copy.wait()
-
-
-def fetch(tile):
-    return pl.pallas_call(
-        fetch_kernel,
-        name="fetch",
-        out_shape=pltpu.VMEM(tile.shape, tile.dtype),
-        in_specs=[hbm()],
-        out_specs=vmem(),
-        scratch_shapes=[pltpu.SemaphoreType.DMA((8,))],
-        compiler_params=pltpu.CompilerParams(vmem_limit_bytes=PREPARE_VMEM),
-        cost_estimate=cost(1e6, 4e6),
-    )(pltpu.with_memory_space_constraint(tile, pltpu.HBM))
 
 
 def scalar_of(msg, n):
@@ -528,8 +515,8 @@
     return jnp.concatenate(parts, axis=1)
 
 
-def behind(profile, edge):
-    return jnp.concatenate([profile, jnp.zeros((EXTRA - 2, edge), f32)], axis=0).astype(bf16)
+def behind(profiles, edge):
+    return jnp.concatenate(profiles + [jnp.zeros((EXTRA - 2 * len(profiles), edge), f32)], axis=0).astype(bf16)
 
 
 def own_profiles(mine_ref, theirs_ref):
@@ -546,16 +533,13 @@
     @pl.when(outer)
     def _():
         total = local_pair(msg, profile, beside, tile_ref, mate_ref, win, sem, edge)
-        none = jnp.zeros_like(profile)
-        theirs = [msg[PROFILE : PROFILE + 2], msg[BESIDE : BESIDE + 2], none]
-        denom = weight_sum(msg, theirs + [profile, beside, none])
-        out_ref[0:edge] = (total / denom).astype(bf16)
-        out_ref[edge:] = jnp.zeros((EXTRA, edge), bf16)
+        out_ref[0:edge] = total.astype(bf16)
+        out_ref[edge:] = behind([profile, beside], edge)
 
     @pl.when(jnp.logical_not(outer))
     def _():
         out_ref[0:edge] = contribution(msg, 0, profile, tile_ref, edge).astype(bf16)
-        out_ref[edge:] = behind(profile, edge)
+        out_ref[edge:] = behind([profile], edge)
 
 
 def second_kernel(down_ref, mine_ref, theirs_ref, tile_ref, mate_ref, out_ref, win, sem):
@@ -568,7 +552,7 @@
     def _():
         copy = window_copy(msg, 0, mate_ref, win, sem)
         out_ref[0:edge] = contribution(msg, 0, beside, win, edge, copy).astype(bf16)
-        out_ref[edge:] = behind(beside, edge)
+        out_ref[edge:] = behind([beside], edge)
 
     @pl.when(jnp.logical_not(outer))
     def _():
@@ -606,13 +590,14 @@
     outer = is_outer()
     profile, beside = own_profiles(mine_ref, theirs_ref)
     got, down = got_ref[...].astype(f32), down_ref[...].astype(f32)
-    msg = jnp.where(outer, got, down)
-    theirs = [msg[PROFILE : PROFILE + 2], msg[BESIDE : BESIDE + 2], got[PROFILE : PROFILE + 2]]
+    rows = early_ref[edge:].astype(f32)
+    opposite = jnp.where(outer, rows[0:2], down[PROFILE : PROFILE + 2])
+    opposite_beside = jnp.where(outer, rows[2:4], down[BESIDE : BESIDE + 2])
+    theirs = [opposite, opposite_beside, got[PROFILE : PROFILE + 2]]
     mine_across = side_ref[edge:].astype(f32)[0:2]
     denom = weight_sum(mine_ref[...].astype(f32), [profile, beside, mine_across] + theirs)
-    total = local_ref[...] + side_ref[0:edge].astype(f32)
     early = jnp.where(outer, early_ref[0:edge].astype(f32), 0.0)
-    block = total / denom + early
+    block = (local_ref[...] + side_ref[0:edge].astype(f32) + early) / denom
     out_ref[...] = block
     pooled_ref[...] = (pool(block.astype(bf16), half) + pooled_early_ref[...].astype(f32)).astype(bf16)
 
@@ -663,7 +648,7 @@
     across_outer = swap([(0, 3), (4, 7)])
     outer_to_inner = [(0, 2), (3, 1), (4, 6), (7, 5)]
 
-    mine, diag, aside, own_msg = prepare(
+    asked, mine, aside, own_msg, near = prepare(
         row_taps[0, 0],
         col_taps[0, 0],
         row_starts.reshape(-1, 1, edge),
@@ -672,16 +657,15 @@
         offsets[0, 0].T,
         feather_rows[0],
         feather_cols[0],
+        tile,
     )
+    mate = send(tile, in_chip)
+    outer = is_outer()
+    got = send(asked, vertical_outer + diagonal)
     theirs = send(aside, in_chip)
-    theirs, tile_after = lax.optimization_barrier((theirs, tile))
-    mate = send(tile_after, in_chip)
-    near = fetch(tile)
-    outer = is_outer()
     row = lax.broadcasted_iota(jnp.int32, mine.shape, 0)
     from_beside = jnp.logical_and(row >= BESIDE, row < BESIDE + 2)
     asking = jnp.where(from_beside, theirs, mine)
-    got = send(jnp.where(outer, asking, diag), vertical_outer + diagonal)
     down = send(jnp.where(outer, theirs, asking), across_outer + vertical_inner)
 
     block = jax.ShapeDtypeStruct((edge + EXTRA, edge), bf16)

time: 48.1 us -> 47 us (0.977); the launches traced: 47.9 us -> 46 us
  Pallas kernels: 14.4 us -> 13.5 us
  waiting for transfers between devices: 15.6 us -> 14.7 us
    pallas_call x1 -> x0, Pallas kernels: 1.57 us -> none  [fetch(): pl.pallas_call(fetch_kernel, name='fetch', out_shape=pltpu.VMEM(tile.shap...]
    ppermute x8, waiting for transfers between devices: 10.4 us -> 9.47 us  [send(): return lax.ppermute(value, 'blk', pairs)]
    pallas_call x1, Pallas kernels: 0.98 us -> 1.71 us  [prepare(): pl.pallas_call(prepare_kernel, name='prepare', out_shape=[jax.ShapeDtypeS...]
  transfers between devices with their start and end apart: 10 -> 10, of which waited for: 6 -> 7; matrix products, arithmetic and copies ran while one was open for 2% -> 2% of each run, Pallas kernels for 26% -> 28%
where the time goes in v4:
time: 47 us; the launch traced here: 46 us
  starting transfers between devices  16.2 us (34%)
  waiting for transfers between devices  14.7 us (31%)
  Pallas kernels  13.5 us (29%)
  other arithmetic  0.81 us (2%)
  between operations  0.74 us (2%)
    pallas_call x6, Pallas kernels, call(): pl.pallas_call(kernel, name=name, out_shape=out_shape, in_specs=[vmem()]...  11.8 us
    ppermute x8, starting transfers between devices, send(): return lax.ppermute(value, 'blk', pairs)  10.4 us
    ppermute x8, waiting for transfers between devices, send(): return lax.ppermute(value, 'blk', pairs)  9.47 us
    ppermute x1, waiting for transfers between devices, two_row_device(): lax.ppermute(pooled_all, 'sec', [(i, i + 1) for i in range(sections - 1)])  4.26 us
    ppermute x1, starting transfers between devices, two_row_device(): lax.ppermute(pooled_all, 'sec', [(i + 1, i) for i in range(sections - 1)])  3.35 us
    ppermute x1, starting transfers between devices, two_row_device(): lax.ppermute(pooled_all, 'sec', [(i, i + 1) for i in range(sections - 1)])  2.5 us
    pallas_call x1, Pallas kernels, prepare(): pl.pallas_call(prepare_kernel, name='prepare', out_shape=[jax.ShapeDtypeS...  1.71 us
    ppermute x1, waiting for transfers between devices, two_row_device(): lax.ppermute(pooled_all, 'sec', [(i + 1, i) for i in range(sections - 1)])  0.99 us
  transfers between devices with their start and end apart: 10, of which 7 were waited for; matrix products, arithmetic and copies ran while one was open for 2% of the time, Pallas kernels for 28%

profile of v4, /device:TPU:28, one launch (start us, length us, event | category | flops | bytes accessed | tf_op | source)
XLA Modules:
  0.0 46.0 jit_solution(9411963262750172862)
XLA Ops:
  0.6 0.1 collective-permute-start.2
  0.7 1.7 %prepare.1 = (bf16[32,512]{1,0:T(8,128)(2,1)S(1)}, bf16[32,512]{1,0:T(8,128)(2,1)S(1)}, bf16[32,512]{1,0:T(8,128)(2,1)S(1)}, bf16[32,512]{1,0:T(8,128)(2,1)S(1)}, bf16[1024,1024]{1,0:T(8,128)(2,1)S(1)}) custom-call(bf16[9,4,512]{2,1,0:T(4,128)(2,1)} %bitcast.17, bf16[9,4,512]{2,1,0:T(4,128)(2,1)} %bitcast.18, s32[9,1,512]{2,1,0:T(1,128)} %bitcast.19, ...), custom_call_target="tpu_custom_call" | custom-call | flops 1000000 | bytes 200000 | tf_op jit(solution)/shard_map/prepare/pallas_call | solution.py:439
  2.4 0.4 collective-permute-start
  2.8 0.3 collective-permute-start.1
  3.1 1.8 %collective-permute-done.1.theirs_ref = bf16[32,512]{1,0:T(8,128)(2,1)S(1)} collective-permute-done((bf16[32,512]{1,0:T(8,128)(2,1)S(1)}, bf16[32,512]{1,0:T(8,128)(2,1)S(1)}, u32[]{:S(2)}, u32[]{:S(2)}) %collective-permute-start.1) | collective-permute-done | bytes 32800 | tf_op jit(solution)/shard_map/ppermute | solution.py:638
  4.9 0.1 select_select_fusion
  5.0 1.6 %collective-permute-start.4 = (bf16[32,512]{1,0:T(8,128)(2,1)S(1)}, bf16[32,512]{1,0:T(8,128)(2,1)S(1)}, u32[]{:S(2)}, u32[]{:S(2)}) collective-permute-start(bf16[32,512]{1,0:T(8,128)(2,1)S(1)} %select_select_fusion), channel_id=1, source_target_pairs={{0,3},{4,7},{3,0},{7,4},{1,5},{2,6},{5,1},{6,2},{8,11},{12,15},{11... | collective-permute-start | bytes 98312 | tf_op jit(solution)/shard_map/ppermute | solution.py:638
  6.6 1.1 %collective-permute-done.got_ref = bf16[32,512]{1,0:T(8,128)(2,1)S(1)} collective-permute-done((bf16[32,512]{1,0:T(8,128)(2,1)S(1)}, bf16[32,512]{1,0:T(8,128)(2,1)S(1)}, u32[]{:S(2)}, u32[]{:S(2)}) %collective-permute-start) | collective-permute-done | bytes 32800 | tf_op jit(solution)/shard_map/ppermute | solution.py:638
  7.6 0.0 collective-permute-done.2.mate_ref
  7.6 1.7 %first.1 = bf16[528,512]{1,0:T(8,128)(2,1)S(1)} custom-call(bf16[32,512]{1,0:T(8,128)(2,1)S(1)} %collective-permute-done.got_ref, bf16[32,512]{1,0:T(8,128)(2,1)S(1)} %get-tuple-element.19.mine_ref, bf16[32,512]{1,0:T(8,128)(2,1)S(1)} %collective-permute-done.1.theirs_ref, bf16[1024,1024]{1,0:T(8,128)(2,1)S(1)} %get-tuple-element.21.tile_ref, ...), custom_call_target="tpu_custom_call" | custom-call | flops 10000 | bytes 10000 | tf_op jit(solution)/shard_map/first/pallas_call | solution.py:618
  9.3 0.1 collective-permute-start.3
  9.4 0.4 collective-permute-done.4.down_ref
  9.8 4.1 %second.1.local_ref = bf16[528,512]{1,0:T(8,128)(2,1)S(1)} custom-call(bf16[32,512]{1,0:T(8,128)(2,1)S(1)} %collective-permute-done.4.down_ref, bf16[32,512]{1,0:T(8,128)(2,1)S(1)} %get-tuple-element.19.mine_ref, bf16[32,512]{1,0:T(8,128)(2,1)S(1)} %collective-permute-done.1.theirs_ref, bf16[1024,1024]{1,0:T(8,128)(2,1)S(1)} %get-tuple-element.21.tile_ref, ...), custom_call_target="tpu_custom_call" | custom-call | flops 4000000000 | bytes 4000000 | tf_op jit(solution)/shard_map/second/pallas_call | solution.py:618
  13.9 4.0 %own.1.local_ref = f32[512,512]{1,0:T(8,128)S(1)} custom-call(bf16[32,512]{1,0:T(8,128)(2,1)S(1)} %get-tuple-element.25.own_ref, bf16[32,512]{1,0:T(8,128)(2,1)S(1)} %get-tuple-element.19.mine_ref, bf16[32,512]{1,0:T(8,128)(2,1)S(1)} %collective-permute-done.1.theirs_ref, bf16[1024,1024]{1,0:T(8,128)(2,1)S(1)} %get-tuple-element.21.tile_ref, ...), custom_call_target="tpu_custom_call" | custom-call | flops 4000000000 | bytes 4000000 | tf_op jit(solution)/shard_map/own/pallas_call | solution.py:618
  17.9 1.3 %collective-permute-start.5 = (bf16[528,512]{1,0:T(8,128)(2,1)S(1)}, bf16[528,512]{1,0:T(8,128)(2,1)S(1)}, u32[]{:S(2)}, u32[]{:S(2)}) collective-permute-start(bf16[528,512]{1,0:T(8,128)(2,1)S(1)} %second.1.local_ref), channel_id=1, source_target_pairs={{0,2},{3,1},{4,6},{7,5},{8,10},{11,9},{12,14},{15,13},{16,18},{19,... | collective-permute-start | bytes 1622024 | tf_op jit(solution)/shard_map/ppermute | solution.py:638
  19.2 2.8 %collective-permute-done.3.over_ref.early_ref = bf16[528,512]{1,0:T(8,128)(2,1)S(1)} collective-permute-done((bf16[528,512]{1,0:T(8,128)(2,1)S(1)}, bf16[528,512]{1,0:T(8,128)(2,1)S(1)}, u32[]{:S(2)}, u32[]{:S(2)}) %collective-permute-start.3) | collective-permute-done | bytes 540704 | tf_op jit(solution)/shard_map/ppermute | solution.py:638
  22.0 0.6 %merge.1 = (bf16[512,512]{1,0:T(8,128)(2,1)S(1)}, bf16[256,256]{1,0:T(8,128)(2,1)S(1)}) custom-call(bf16[528,512]{1,0:T(8,128)(2,1)S(1)} %second.1.local_ref, bf16[528,512]{1,0:T(8,128)(2,1)S(1)} %collective-permute-done.3.over_ref.early_ref, bf16[32,512]{1,0:T(8,128)(2,1)S(1)} %collective-permute-done.got_ref, ...), custom_call_target="tpu_custom_call" | custom-call | flops 1000000000 | bytes 4000000 | tf_op jit(solution)/shard_map/merge/pallas_call | solution.py:618
  22.6 1.9 %collective-permute-start.6 = (bf16[256,256]{1,0:T(8,128)(2,1)S(1)}, bf16[256,256]{1,0:T(8,128)(2,1)S(1)}, u32[]{:S(2)}, u32[]{:S(2)}) collective-permute-start(bf16[256,256]{1,0:T(8,128)(2,1)S(1)} %get-tuple-element.30), channel_id=1, source_target_pairs={{1,5},{2,6},{5,1},{6,2},{9,13},{10,14},{13,9},{14,10},{17,21},{18,... | collective-permute-start | bytes 393224 | tf_op jit(solution)/shard_map/ppermute | solution.py:638
  24.5 4.8 %collective-permute-start.7 = (bf16[512,512]{1,0:T(8,128)(2,1)S(1)}, bf16[512,512]{1,0:T(8,128)(2,1)S(1)}, u32[]{:S(2)}, u32[]{:S(2)}) collective-permute-start(bf16[512,512]{1,0:T(8,128)(2,1)S(1)} %get-tuple-element.32), channel_id=1, source_target_pairs={{1,5},{2,6},{5,1},{6,2},{9,13},{10,14},{13,9},{14,10},{17,21},{18,... | collective-permute-start | bytes 1572872 | tf_op jit(solution)/shard_map/ppermute | solution.py:638
  29.3 3.4 %collective-permute-done.5.side_ref = bf16[528,512]{1,0:T(8,128)(2,1)S(1)} collective-permute-done((bf16[528,512]{1,0:T(8,128)(2,1)S(1)}, bf16[528,512]{1,0:T(8,128)(2,1)S(1)}, u32[]{:S(2)}, u32[]{:S(2)}) %collective-permute-start.5) | collective-permute-done | bytes 540704 | tf_op jit(solution)/shard_map/ppermute | solution.py:638
  32.7 0.0 collective-permute-done.6.pooled_early_ref
  32.7 0.6 %blend.1 = (f32[512,512]{1,0:T(8,128)S(1)}, bf16[256,256]{1,0:T(8,128)(2,1)S(1)}) custom-call(f32[512,512]{1,0:T(8,128)S(1)} %own.1.local_ref, bf16[528,512]{1,0:T(8,128)(2,1)S(1)} %collective-permute-done.5.side_ref, bf16[32,512]{1,0:T(8,128)(2,1)S(1)} %collective-permute-done.got_ref, bf16[32,512]{1,0:T(8,128)(2,1)S(1)} %collective-permute-done.4.down_ref, ...), custom_call_target="tpu_custom_call" | custom-call | flops 1000000000 | bytes 4000000 | tf_op jit(solution)/shard_map/blend/pallas_call | solution.py:618
  33.3 3.4 %collective-permute-start.9 = (bf16[256,256]{1,0:T(8,128)(2,1)S(1)}, bf16[256,256]{1,0:T(8,128)(2,1)S(1)}, u32[]{:S(2)}, u32[]{:S(2)}) collective-permute-start(bf16[256,256]{1,0:T(8,128)(2,1)S(1)} %get-tuple-element.33), channel_id=1, source_target_pairs={{8,0},{16,8},{24,16},{9,1},{17,9},{25,17},{10,2},{18,10},{26,18},{... | collective-permute-start | bytes 393224 | tf_op jit(solution)/shard_map/ppermute | solution.py:701
  36.7 2.5 %collective-permute-start.8 = (bf16[256,256]{1,0:T(8,128)(2,1)S(1)}, bf16[256,256]{1,0:T(8,128)(2,1)S(1)}, u32[]{:S(2)}, u32[]{:S(2)}) collective-permute-start(bf16[256,256]{1,0:T(8,128)(2,1)S(1)} %get-tuple-element.33), channel_id=1, source_target_pairs={{0,8},{8,16},{16,24},{1,9},{9,17},{17,25},{2,10},{10,18},{18,26},{... | collective-permute-start | bytes 393224 | tf_op jit(solution)/shard_map/ppermute | solution.py:700
  39.2 1.0 %collective-permute-done.9 = bf16[256,256]{1,0:T(8,128)(2,1)S(1)} collective-permute-done((bf16[256,256]{1,0:T(8,128)(2,1)S(1)}, bf16[256,256]{1,0:T(8,128)(2,1)S(1)}, u32[]{:S(2)}, u32[]{:S(2)}) %collective-permute-start.9) | collective-permute-done | bytes 131104 | tf_op jit(solution)/shard_map/ppermute | solution.py:701
  40.2 4.3 %collective-permute-done.8 = bf16[256,256]{1,0:T(8,128)(2,1)S(1)} collective-permute-done((bf16[256,256]{1,0:T(8,128)(2,1)S(1)}, bf16[256,256]{1,0:T(8,128)(2,1)S(1)}, u32[]{:S(2)}, u32[]{:S(2)}) %collective-permute-start.8) | collective-permute-done | bytes 131104 | tf_op jit(solution)/shard_map/ppermute | solution.py:700
  44.4 0.7 %fusion = bf16[1,1,256,256]{3,2,1,0:T(8,128)(2,1)} fusion(f32[]{:T(128)S(6)} %sub.7, bf16[256,256]{1,0:T(8,128)(2,1)S(1)} %collective-permute-done.9, bf16[256,256]{1,0:T(8,128)(2,1)S(1)} %get-tuple-element.33, bf16[256,256]{1,0:T(8,128)(2,1)S(1)} %collective-permute-done.8), kind=kLoop, calls=%fused_computation.1 | loop fusion | flops 524288 | bytes 524292 | tf_op jit(solution)/shard_map/broadcast_in_dim | solution.py:706
  45.2 0.0 collective-permute-done.7.late_ref
  45.2 0.9 %last.1 = bf16[512,512]{1,0:T(8,128)(2,1)} custom-call(f32[512,512]{1,0:T(8,128)S(1)} %get-tuple-element.31.block_ref, bf16[512,512]{1,0:T(8,128)(2,1)S(1)} %collective-permute-done.7.late_ref), custom_call_target="tpu_custom_call" | custom-call | flops 1000000 | bytes 2000000 | tf_op jit(solution)/shard_map/last/pallas_call | solution.py:618
  (1 shorter events, 0.0 us)
Async XLA Ops:
  0.6 7.0 %collective-permute-start.2 = (bf16[1024,1024]{1,0:T(8,128)(2,1)}, bf16[1024,1024]{1,0:T(8,128)(2,1)}, u32[]{:S(2)}, u32[]{:S(2)}) collective-permute-start(bf16[1024,1024]{1,0:T(8,128)(2,1)} %bitcast.14), channel_id=1, source_target_pairs={{0,1},{1,0},{2,3},{3,2},{4,5},{5,4},{6,7},{7,6},{8,9},{9,8},{10,11... | collective-permute-start | bytes 6291464 | tf_op jit(solution)/shard_map/ppermute | solution.py:638
  2.4 5.2 %collective-permute-start = (bf16[32,512]{1,0:T(8,128)(2,1)S(1)}, bf16[32,512]{1,0:T(8,128)(2,1)S(1)}, u32[]{:S(2)}, u32[]{:S(2)}) collective-permute-start(bf16[32,512]{1,0:T(8,128)(2,1)S(1)} %get-tuple-element.18), channel_id=1, source_target_pairs={{0,4},{3,7},{4,0},{7,3},{1,6},{2,5},{6,1},{5,2},{8,12},{11,15},{12... | collective-permute-start | bytes 98312 | tf_op jit(solution)/shard_map/ppermute | solution.py:638
  2.8 2.1 %collective-permute-start.1 = (bf16[32,512]{1,0:T(8,128)(2,1)S(1)}, bf16[32,512]{1,0:T(8,128)(2,1)S(1)}, u32[]{:S(2)}, u32[]{:S(2)}) collective-permute-start(bf16[32,512]{1,0:T(8,128)(2,1)S(1)} %get-tuple-element.20), channel_id=1, source_target_pairs={{0,1},{1,0},{2,3},{3,2},{4,5},{5,4},{6,7},{7,6},{8,9},{9,8},{10,11... | collective-permute-start | bytes 98312 | tf_op jit(solution)/shard_map/ppermute | solution.py:638
  5.0 4.8 %collective-permute-start.4 = (bf16[32,512]{1,0:T(8,128)(2,1)S(1)}, bf16[32,512]{1,0:T(8,128)(2,1)S(1)}, u32[]{:S(2)}, u32[]{:S(2)}) collective-permute-start(bf16[32,512]{1,0:T(8,128)(2,1)S(1)} %select_select_fusion), channel_id=1, source_target_pairs={{0,3},{4,7},{3,0},{7,4},{1,5},{2,6},{5,1},{6,2},{8,11},{12,15},{11... | collective-permute-start | bytes 98312 | tf_op jit(solution)/shard_map/ppermute | solution.py:638
  9.3 12.7 %collective-permute-start.3 = (bf16[528,512]{1,0:T(8,128)(2,1)S(1)}, bf16[528,512]{1,0:T(8,128)(2,1)S(1)}, u32[]{:S(2)}, u32[]{:S(2)}) collective-permute-start(bf16[528,512]{1,0:T(8,128)(2,1)S(1)} %first.1), channel_id=1, source_target_pairs={{0,4},{3,7},{4,0},{7,3},{1,2},{5,6},{2,1},{6,5},{8,12},{11,15},{12... | collective-permute-start | bytes 1622024 | tf_op jit(solution)/shard_map/ppermute | solution.py:638
  17.9 14.8 %collective-permute-start.5 = (bf16[528,512]{1,0:T(8,128)(2,1)S(1)}, bf16[528,512]{1,0:T(8,128)(2,1)S(1)}, u32[]{:S(2)}, u32[]{:S(2)}) collective-permute-start(bf16[528,512]{1,0:T(8,128)(2,1)S(1)} %second.1.local_ref), channel_id=1, source_target_pairs={{0,2},{3,1},{4,6},{7,5},{8,10},{11,9},{12,14},{15,13},{16,18},{19,... | collective-permute-start | bytes 1622024 | tf_op jit(solution)/shard_map/ppermute | solution.py:638
  22.6 10.1 %collective-permute-start.6 = (bf16[256,256]{1,0:T(8,128)(2,1)S(1)}, bf16[256,256]{1,0:T(8,128)(2,1)S(1)}, u32[]{:S(2)}, u32[]{:S(2)}) collective-permute-start(bf16[256,256]{1,0:T(8,128)(2,1)S(1)} %get-tuple-element.30), channel_id=1, source_target_pairs={{1,5},{2,6},{5,1},{6,2},{9,13},{10,14},{13,9},{14,10},{17,21},{18,... | collective-permute-start | bytes 393224 | tf_op jit(solution)/shard_map/ppermute | solution.py:638
  24.5 20.7 %collective-permute-start.7 = (bf16[512,512]{1,0:T(8,128)(2,1)S(1)}, bf16[512,512]{1,0:T(8,128)(2,1)S(1)}, u32[]{:S(2)}, u32[]{:S(2)}) collective-permute-start(bf16[512,512]{1,0:T(8,128)(2,1)S(1)} %get-tuple-element.32), channel_id=1, source_target_pairs={{1,5},{2,6},{5,1},{6,2},{9,13},{10,14},{13,9},{14,10},{17,21},{18,... | collective-permute-start | bytes 1572872 | tf_op jit(solution)/shard_map/ppermute | solution.py:638
  33.3 6.9 %collective-permute-start.9 = (bf16[256,256]{1,0:T(8,128)(2,1)S(1)}, bf16[256,256]{1,0:T(8,128)(2,1)S(1)}, u32[]{:S(2)}, u32[]{:S(2)}) collective-permute-start(bf16[256,256]{1,0:T(8,128)(2,1)S(1)} %get-tuple-element.33), channel_id=1, source_target_pairs={{8,0},{16,8},{24,16},{9,1},{17,9},{25,17},{10,2},{18,10},{26,18},{... | collective-permute-start | bytes 393224 | tf_op jit(solution)/shard_map/ppermute | solution.py:701
  36.7 7.8 %collective-permute-start.8 = (bf16[256,256]{1,0:T(8,128)(2,1)S(1)}, bf16[256,256]{1,0:T(8,128)(2,1)S(1)}, u32[]{:S(2)}, u32[]{:S(2)}) collective-permute-start(bf16[256,256]{1,0:T(8,128)(2,1)S(1)} %get-tuple-element.33), channel_id=1, source_target_pairs={{0,8},{8,16},{16,24},{1,9},{9,17},{17,25},{2,10},{10,18},{18,26},{... | collective-permute-start | bytes 393224 | tf_op jit(solution)/shard_map/ppermute | solution.py:700

commit v5 on v4

--- a/solution.py
+++ b/solution.py
@@ -467,7 +467,7 @@
     return copy
 
 
-def contribution(msg, half, profile, tile_ref, edge, copy=None):
+def contribution(msg, half, profile, tile_ref, edge, copy=None, parts=1):
     prm = msg[half * HALF : half * HALF + HALF]
     prm = jnp.concatenate([prm, profile, jnp.zeros((2, edge), f32)], axis=0)
     rmat = row_matrix(prm, edge)
@@ -477,15 +477,20 @@
     else:
         copy.wait()
         window = tile_ref[...]
-    rows = jnp.dot(rmat, window, preferred_element_type=f32).astype(bf16)
-    contrib = jnp.dot(rows, cmat, preferred_element_type=f32)
-    return contrib * prm.T[:, HALF : HALF + 1] * profile[1:2]
-
-
-def local_pair(msg, profile, beside, tile_ref, mate_ref, win, sem, edge):
+    weight = prm.T[:, HALF : HALF + 1]
+    total = []
+    for n in range(parts):
+        part = slice(n * edge // parts, (n + 1) * edge // parts)
+        rows = jnp.dot(rmat[part], window, preferred_element_type=f32).astype(bf16)
+        contrib = jnp.dot(rows, cmat, preferred_element_type=f32)
+        total.append(contrib * weight[part] * profile[1:2])
+    return jnp.concatenate(total, axis=0) if parts > 1 else total[0]
+
+
+def local_pair(msg, profile, beside, tile_ref, mate_ref, win, sem, edge, parts=1):
     copy = window_copy(msg, 1, mate_ref, win, sem)
-    total = contribution(msg, 0, profile, tile_ref, edge)
-    return total + contribution(msg, 1, beside, win, edge, copy)
+    total = contribution(msg, 0, profile, tile_ref, edge, None, parts)
+    return total + contribution(msg, 1, beside, win, edge, copy, parts)
 
 
 def weight_sum(msg, profiles):
@@ -532,7 +537,7 @@
 
     @pl.when(outer)
     def _():
-        total = local_pair(msg, profile, beside, tile_ref, mate_ref, win, sem, edge)
+        total = local_pair(msg, profile, beside, tile_ref, mate_ref, win, sem, edge, 2)
         out_ref[0:edge] = total.astype(bf16)
         out_ref[edge:] = behind([profile, beside], edge)
 
@@ -556,7 +561,7 @@
 
     @pl.when(jnp.logical_not(outer))
     def _():
-        total = local_pair(msg, profile, beside, tile_ref, mate_ref, win, sem, edge)
+        total = local_pair(msg, profile, beside, tile_ref, mate_ref, win, sem, edge, 4)
         out_ref[0:edge] = total.astype(bf16)
         out_ref[edge:] = jnp.zeros((EXTRA, edge), bf16)
 
@@ -580,7 +585,7 @@
 def own_kernel(own_ref, mine_ref, theirs_ref, tile_ref, mate_ref, out_ref, win, sem):
     profile, beside = own_profiles(mine_ref, theirs_ref)
     msg = own_ref[...].astype(f32)
-    out_ref[...] = local_pair(msg, profile, beside, tile_ref, mate_ref, win, sem, out_ref.shape[1])
+    out_ref[...] = local_pair(msg, profile, beside, tile_ref, mate_ref, win, sem, out_ref.shape[1], 4)
 
 
 def blend_kernel(
@@ -602,8 +607,40 @@
     pooled_ref[...] = (pool(block.astype(bf16), half) + pooled_early_ref[...].astype(f32)).astype(bf16)
 
 
-def last_kernel(block_ref, late_ref, out_ref):
-    out_ref[...] = (block_ref[...] + late_ref[...].astype(f32)).astype(bf16)
+def last_kernel(block_ref, late_ref, before_ref, after_ref, pooled_ref, out_hbm, level_hbm, out_buf, level_buf, sems):
+    index, sections = lax.axis_index("sec"), lax.axis_size("sec")
+    ends = (index == 0).astype(jnp.int32) + (index == sections - 1).astype(jnp.int32)
+    present = 4.0 - ends.astype(f32)
+    total = before_ref[...].astype(f32) + 2.0 * pooled_ref[...].astype(f32) + after_ref[...].astype(f32)
+    level_buf[...] = (total / present).astype(bf16)
+    copies = [pltpu.make_async_copy(level_buf, level_hbm, sems.at[PARTS])]
+    copies[0].start()
+    size = block_ref.shape[0] // PARTS
+    for n in range(PARTS):
+        rows = slice(n * size, (n + 1) * size)
+        out_buf[rows] = (block_ref[rows] + late_ref[rows].astype(f32)).astype(bf16)
+        copies.append(pltpu.make_async_copy(out_buf.at[rows], out_hbm.at[rows], sems.at[n]))
+        copies[-1].start()
+    for copy in copies:
+        copy.wait()
+
+
+PARTS = 4
+
+
+def last(block, late, before, after, pooled):
+    shapes = [jax.ShapeDtypeStruct(block.shape, bf16), jax.ShapeDtypeStruct(pooled.shape, bf16)]
+    args = [pltpu.with_memory_space_constraint(x, pltpu.VMEM) for x in (block, late, before, after, pooled)]
+    return pl.pallas_call(
+        last_kernel,
+        name="last",
+        out_shape=shapes,
+        in_specs=[vmem()] * 5,
+        out_specs=[hbm()] * 2,
+        scratch_shapes=[pltpu.VMEM(x.shape, x.dtype) for x in shapes] + [pltpu.SemaphoreType.DMA((PARTS + 1,))],
+        compiler_params=pltpu.CompilerParams(vmem_limit_bytes=WORK_VMEM),
+        cost_estimate=cost(1e6, 2e6),
+    )(*args)
 
 
 def call(kernel, name, out_shape, operands, mate=None, halves=False, work=(1e9, 4e6)):
@@ -695,15 +732,14 @@
         [bare32, pooled],
         (local, side, got, down, mine, theirs, early, pooled_late),
         halves=True,
+        work=(5175000000.0, 1e6),
     )
     sections = lax.axis_size("sec")
     before = lax.ppermute(pooled_all, "sec", [(i, i + 1) for i in range(sections - 1)])
     after = lax.ppermute(pooled_all, "sec", [(i + 1, i) for i in range(sections - 1)])
-    blended = call(last_kernel, "last", bare, (block_so_far, late), work=(1e6, 2e6))
-    index = lax.axis_index("sec")
-    present = 4.0 - (index == 0).astype(f32) - (index == sections - 1).astype(f32)
-    level = (before.astype(f32) + 2.0 * pooled_all.astype(f32) + after.astype(f32)) / present
-    return blended[None, None], level.astype(bf16)[None, None]
+    after, late = lax.optimization_barrier((after, late))
+    blended, level = last(block_so_far, late, before, after, pooled_all)
+    return blended[None, None], level[None, None]
 
 
 def per_device(*args):

time: 47 us -> 46.5 us (0.989)
  other arithmetic: 0.81 us -> 0.08 us
  Pallas kernels: 13.5 us -> 14.2 us
    ppermute x1, waiting for transfers between devices: 4.26 us -> 1.86 us  [two_row_device(): lax.ppermute(pooled_all, 'sec', [(i, i + 1) for i in range(sections - 1)])]
    ppermute x8, waiting for transfers between devices: 9.47 us -> 11.7 us  [send(): return lax.ppermute(value, 'blk', pairs)]
    pallas_call x0 -> x1, Pallas kernels: none -> 0.94 us  [last(): pl.pallas_call(last_kernel, name='last', out_shape=shapes, in_specs=[vmem...]
    broadcast_in_dim x1 -> x0, other arithmetic: 0.72 us -> none  [two_row_device(): return (blended[None, None], level.astype(bf16)[None, None])]
    pallas_call x6 -> x5, Pallas kernels: 11.8 us -> 11.5 us  [call(): pl.pallas_call(kernel, name=name, out_shape=out_shape, in_specs=[vmem()]...]
  transfers between devices with their start and end apart: 10 -> 10, of which waited for: 7 -> 8; matrix products, arithmetic and copies ran while one was open for 2% -> 0% of each run, Pallas kernels for 28% -> 29%
where the time goes in v5:
time: 46.5 us; the launch traced here: 46 us
  starting transfers between devices  16.2 us (35%)
  waiting for transfers between devices  14.6 us (31%)
  Pallas kernels  14.2 us (31%)
  between operations  0.89 us (2%)
    ppermute x8, waiting for transfers between devices, send(): return lax.ppermute(value, 'blk', pairs)  11.7 us
    pallas_call x5, Pallas kernels, call(): pl.pallas_call(kernel, name=name, out_shape=out_shape, in_specs=[vmem()]...  11.5 us
    ppermute x8, starting transfers between devices, send(): return lax.ppermute(value, 'blk', pairs)  10.4 us
    ppermute x1, starting transfers between devices, two_row_device(): lax.ppermute(pooled_all, 'sec', [(i + 1, i) for i in range(sections - 1)])  3.39 us
    ppermute x1, starting transfers between devices, two_row_device(): lax.ppermute(pooled_all, 'sec', [(i, i + 1) for i in range(sections - 1)])  2.45 us
    ppermute x1, waiting for transfers between devices, two_row_device(): lax.ppermute(pooled_all, 'sec', [(i, i + 1) for i in range(sections - 1)])  1.86 us
    pallas_call x1, Pallas kernels, prepare(): pl.pallas_call(prepare_kernel, name='prepare', out_shape=[jax.ShapeDtypeS...  1.71 us
    ppermute x1, waiting for transfers between devices, two_row_device(): lax.ppermute(pooled_all, 'sec', [(i + 1, i) for i in range(sections - 1)])  1 us
  transfers between devices with their start and end apart: 10, of which 8 were waited for; matrix products, arithmetic and copies ran while one was open for 0% of the time, Pallas kernels for 29%

profile of v5, /device:TPU:28, one launch (start us, length us, event | category | flops | bytes accessed | tf_op | source)
XLA Modules:
  0.0 46.0 jit_solution(7887062139512608348)
XLA Ops:
  0.6 0.1 collective-permute-start.2
  0.7 1.7 %prepare.1 = (bf16[32,512]{1,0:T(8,128)(2,1)S(1)}, bf16[32,512]{1,0:T(8,128)(2,1)S(1)}, bf16[32,512]{1,0:T(8,128)(2,1)S(1)}, bf16[32,512]{1,0:T(8,128)(2,1)S(1)}, bf16[1024,1024]{1,0:T(8,128)(2,1)S(1)}) custom-call(bf16[9,4,512]{2,1,0:T(4,128)(2,1)} %bitcast.15, bf16[9,4,512]{2,1,0:T(4,128)(2,1)} %bitcast.16, s32[9,1,512]{2,1,0:T(1,128)} %bitcast.17, ...), custom_call_target="tpu_custom_call" | custom-call | flops 1000000 | bytes 200000 | tf_op jit(solution)/shard_map/prepare/pallas_call | solution.py:439
  2.4 0.4 collective-permute-start
  2.8 0.3 collective-permute-start.1
  3.1 1.8 %collective-permute-done.1.theirs_ref = bf16[32,512]{1,0:T(8,128)(2,1)S(1)} collective-permute-done((bf16[32,512]{1,0:T(8,128)(2,1)S(1)}, bf16[32,512]{1,0:T(8,128)(2,1)S(1)}, u32[]{:S(2)}, u32[]{:S(2)}) %collective-permute-start.1) | collective-permute-done | bytes 32800 | tf_op jit(solution)/shard_map/ppermute | solution.py:675
  4.9 0.1 select_select_fusion
  5.0 1.6 %collective-permute-start.4 = (bf16[32,512]{1,0:T(8,128)(2,1)S(1)}, bf16[32,512]{1,0:T(8,128)(2,1)S(1)}, u32[]{:S(2)}, u32[]{:S(2)}) collective-permute-start(bf16[32,512]{1,0:T(8,128)(2,1)S(1)} %select_select_fusion), channel_id=1, source_target_pairs={{0,3},{4,7},{3,0},{7,4},{1,5},{2,6},{5,1},{6,2},{8,11},{12,15},{11... | collective-permute-start | bytes 98312 | tf_op jit(solution)/shard_map/ppermute | solution.py:675
  6.6 1.1 %collective-permute-done.got_ref = bf16[32,512]{1,0:T(8,128)(2,1)S(1)} collective-permute-done((bf16[32,512]{1,0:T(8,128)(2,1)S(1)}, bf16[32,512]{1,0:T(8,128)(2,1)S(1)}, u32[]{:S(2)}, u32[]{:S(2)}) %collective-permute-start) | collective-permute-done | bytes 32800 | tf_op jit(solution)/shard_map/ppermute | solution.py:675
  7.6 0.0 collective-permute-done.2.mate_ref
  7.6 1.7 %first.1 = bf16[528,512]{1,0:T(8,128)(2,1)S(1)} custom-call(bf16[32,512]{1,0:T(8,128)(2,1)S(1)} %collective-permute-done.got_ref, bf16[32,512]{1,0:T(8,128)(2,1)S(1)} %get-tuple-element.23.mine_ref, bf16[32,512]{1,0:T(8,128)(2,1)S(1)} %collective-permute-done.1.theirs_ref, bf16[1024,1024]{1,0:T(8,128)(2,1)S(1)} %get-tuple-element.25.tile_ref, ...), custom_call_target="tpu_custom_call" | custom-call | flops 10000 | bytes 10000 | tf_op jit(solution)/shard_map/first/pallas_call | solution.py:655
  9.3 0.1 collective-permute-start.3
  9.4 0.4 collective-permute-done.4.down_ref
  9.8 4.4 %second.1.local_ref = bf16[528,512]{1,0:T(8,128)(2,1)S(1)} custom-call(bf16[32,512]{1,0:T(8,128)(2,1)S(1)} %collective-permute-done.4.down_ref, bf16[32,512]{1,0:T(8,128)(2,1)S(1)} %get-tuple-element.23.mine_ref, bf16[32,512]{1,0:T(8,128)(2,1)S(1)} %collective-permute-done.1.theirs_ref, bf16[1024,1024]{1,0:T(8,128)(2,1)S(1)} %get-tuple-element.25.tile_ref, ...), custom_call_target="tpu_custom_call" | custom-call | flops 4000000000 | bytes 4000000 | tf_op jit(solution)/shard_map/second/pallas_call | solution.py:655
  14.2 4.2 %own.1.local_ref = f32[512,512]{1,0:T(8,128)S(1)} custom-call(bf16[32,512]{1,0:T(8,128)(2,1)S(1)} %get-tuple-element.29.own_ref, bf16[32,512]{1,0:T(8,128)(2,1)S(1)} %get-tuple-element.23.mine_ref, bf16[32,512]{1,0:T(8,128)(2,1)S(1)} %collective-permute-done.1.theirs_ref, bf16[1024,1024]{1,0:T(8,128)(2,1)S(1)} %get-tuple-element.25.tile_ref, ...), custom_call_target="tpu_custom_call" | custom-call | flops 4000000000 | bytes 4000000 | tf_op jit(solution)/shard_map/own/pallas_call | solution.py:655
  18.5 1.3 %collective-permute-start.5 = (bf16[528,512]{1,0:T(8,128)(2,1)S(1)}, bf16[528,512]{1,0:T(8,128)(2,1)S(1)}, u32[]{:S(2)}, u32[]{:S(2)}) collective-permute-start(bf16[528,512]{1,0:T(8,128)(2,1)S(1)} %second.1.local_ref), channel_id=1, source_target_pairs={{0,2},{3,1},{4,6},{7,5},{8,10},{11,9},{12,14},{15,13},{16,18},{19,... | collective-permute-start | bytes 1622024 | tf_op jit(solution)/shard_map/ppermute | solution.py:675
  19.8 2.5 %collective-permute-done.3.over_ref.early_ref = bf16[528,512]{1,0:T(8,128)(2,1)S(1)} collective-permute-done((bf16[528,512]{1,0:T(8,128)(2,1)S(1)}, bf16[528,512]{1,0:T(8,128)(2,1)S(1)}, u32[]{:S(2)}, u32[]{:S(2)}) %collective-permute-start.3) | collective-permute-done | bytes 540704 | tf_op jit(solution)/shard_map/ppermute | solution.py:675
  22.3 0.6 %merge.1 = (bf16[512,512]{1,0:T(8,128)(2,1)S(1)}, bf16[256,256]{1,0:T(8,128)(2,1)S(1)}) custom-call(bf16[528,512]{1,0:T(8,128)(2,1)S(1)} %second.1.local_ref, bf16[528,512]{1,0:T(8,128)(2,1)S(1)} %collective-permute-done.3.over_ref.early_ref, bf16[32,512]{1,0:T(8,128)(2,1)S(1)} %collective-permute-done.got_ref, ...), custom_call_target="tpu_custom_call" | custom-call | flops 1000000000 | bytes 4000000 | tf_op jit(solution)/shard_map/merge/pallas_call | solution.py:655
  22.9 1.9 %collective-permute-start.6 = (bf16[256,256]{1,0:T(8,128)(2,1)S(1)}, bf16[256,256]{1,0:T(8,128)(2,1)S(1)}, u32[]{:S(2)}, u32[]{:S(2)}) collective-permute-start(bf16[256,256]{1,0:T(8,128)(2,1)S(1)} %get-tuple-element.34), channel_id=1, source_target_pairs={{1,5},{2,6},{5,1},{6,2},{9,13},{10,14},{13,9},{14,10},{17,21},{18,... | collective-permute-start | bytes 393224 | tf_op jit(solution)/shard_map/ppermute | solution.py:675
  24.8 4.8 %collective-permute-start.8 = (bf16[512,512]{1,0:T(8,128)(2,1)S(1)}, bf16[512,512]{1,0:T(8,128)(2,1)S(1)}, u32[]{:S(2)}, u32[]{:S(2)}) collective-permute-start(bf16[512,512]{1,0:T(8,128)(2,1)S(1)} %get-tuple-element.37), channel_id=1, source_target_pairs={{1,5},{2,6},{5,1},{6,2},{9,13},{10,14},{13,9},{14,10},{17,21},{18,... | collective-permute-start | bytes 1572872 | tf_op jit(solution)/shard_map/ppermute | solution.py:675
  29.6 3.4 %collective-permute-done.5.side_ref = bf16[528,512]{1,0:T(8,128)(2,1)S(1)} collective-permute-done((bf16[528,512]{1,0:T(8,128)(2,1)S(1)}, bf16[528,512]{1,0:T(8,128)(2,1)S(1)}, u32[]{:S(2)}, u32[]{:S(2)}) %collective-permute-start.5) | collective-permute-done | bytes 540704 | tf_op jit(solution)/shard_map/ppermute | solution.py:675
  33.1 0.0 collective-permute-done.6.pooled_early_ref
  33.1 0.6 %blend.1 = (f32[512,512]{1,0:T(8,128)S(1)}, bf16[256,256]{1,0:T(8,128)(2,1)S(1)}) custom-call(f32[512,512]{1,0:T(8,128)S(1)} %own.1.local_ref, bf16[528,512]{1,0:T(8,128)(2,1)S(1)} %collective-permute-done.5.side_ref, bf16[32,512]{1,0:T(8,128)(2,1)S(1)} %collective-permute-done.got_ref, bf16[32,512]{1,0:T(8,128)(2,1)S(1)} %collective-permute-done.4.down_ref, ...), custom_call_target="tpu_custom_call" | custom-call | flops 5175000064 | bytes 1000000 | tf_op jit(solution)/shard_map/blend/pallas_call | solution.py:655
  33.7 3.4 %collective-permute-start.7 = (bf16[256,256]{1,0:T(8,128)(2,1)S(1)}, bf16[256,256]{1,0:T(8,128)(2,1)S(1)}, u32[]{:S(2)}, u32[]{:S(2)}) collective-permute-start(bf16[256,256]{1,0:T(8,128)(2,1)S(1)} %get-tuple-element.36.pooled_ref), channel_id=1, source_target_pairs={{8,0},{16,8},{24,16},{9,1},{17,9},{25,17},{10,2},{18,10},{26,18},{... | collective-permute-start | bytes 393224 | tf_op jit(solution)/shard_map/ppermute | solution.py:739
  37.1 2.5 %collective-permute-start.9 = (bf16[256,256]{1,0:T(8,128)(2,1)S(1)}, bf16[256,256]{1,0:T(8,128)(2,1)S(1)}, u32[]{:S(2)}, u32[]{:S(2)}) collective-permute-start(bf16[256,256]{1,0:T(8,128)(2,1)S(1)} %get-tuple-element.36.pooled_ref), channel_id=1, source_target_pairs={{0,8},{8,16},{16,24},{1,9},{9,17},{17,25},{2,10},{10,18},{18,26},{... | collective-permute-start | bytes 393224 | tf_op jit(solution)/shard_map/ppermute | solution.py:738
  39.6 1.0 %collective-permute-done.7.after_ref = bf16[256,256]{1,0:T(8,128)(2,1)S(1)} collective-permute-done((bf16[256,256]{1,0:T(8,128)(2,1)S(1)}, bf16[256,256]{1,0:T(8,128)(2,1)S(1)}, u32[]{:S(2)}, u32[]{:S(2)}) %collective-permute-start.7) | collective-permute-done | bytes 131104 | tf_op jit(solution)/shard_map/ppermute | solution.py:739
  40.6 2.4 %collective-permute-done.8.late_ref = bf16[512,512]{1,0:T(8,128)(2,1)S(1)} collective-permute-done((bf16[512,512]{1,0:T(8,128)(2,1)S(1)}, bf16[512,512]{1,0:T(8,128)(2,1)S(1)}, u32[]{:S(2)}, u32[]{:S(2)}) %collective-permute-start.8) | collective-permute-done | bytes 524320 | tf_op jit(solution)/shard_map/ppermute | solution.py:675
  43.0 1.9 %collective-permute-done.9.before_ref = bf16[256,256]{1,0:T(8,128)(2,1)S(1)} collective-permute-done((bf16[256,256]{1,0:T(8,128)(2,1)S(1)}, bf16[256,256]{1,0:T(8,128)(2,1)S(1)}, u32[]{:S(2)}, u32[]{:S(2)}) %collective-permute-start.9) | collective-permute-done | bytes 131104 | tf_op jit(solution)/shard_map/ppermute | solution.py:738
  44.9 0.9 %last.1 = (bf16[512,512]{1,0:T(8,128)(2,1)}, bf16[256,256]{1,0:T(8,128)(2,1)}) custom-call(f32[512,512]{1,0:T(8,128)S(1)} %get-tuple-element.35.block_ref, bf16[512,512]{1,0:T(8,128)(2,1)S(1)} %collective-permute-done.8.late_ref, bf16[256,256]{1,0:T(8,128)(2,1)S(1)} %collective-permute-done.9.before_ref, ...), custom_call_target="tpu_custom_call" | custom-call | flops 1000000 | bytes 2000000 | tf_op jit(solution)/shard_map/last/pallas_call | solution.py:634
  (1 shorter events, 0.0 us)
Async XLA Ops:
  0.6 7.0 %collective-permute-start.2 = (bf16[1024,1024]{1,0:T(8,128)(2,1)}, bf16[1024,1024]{1,0:T(8,128)(2,1)}, u32[]{:S(2)}, u32[]{:S(2)}) collective-permute-start(bf16[1024,1024]{1,0:T(8,128)(2,1)} %bitcast.13), channel_id=1, source_target_pairs={{0,1},{1,0},{2,3},{3,2},{4,5},{5,4},{6,7},{7,6},{8,9},{9,8},{10,11... | collective-permute-start | bytes 6291464 | tf_op jit(solution)/shard_map/ppermute | solution.py:675
  2.4 5.2 %collective-permute-start = (bf16[32,512]{1,0:T(8,128)(2,1)S(1)}, bf16[32,512]{1,0:T(8,128)(2,1)S(1)}, u32[]{:S(2)}, u32[]{:S(2)}) collective-permute-start(bf16[32,512]{1,0:T(8,128)(2,1)S(1)} %get-tuple-element.22), channel_id=1, source_target_pairs={{0,4},{3,7},{4,0},{7,3},{1,6},{2,5},{6,1},{5,2},{8,12},{11,15},{12... | collective-permute-start | bytes 98312 | tf_op jit(solution)/shard_map/ppermute | solution.py:675
  2.8 2.1 %collective-permute-start.1 = (bf16[32,512]{1,0:T(8,128)(2,1)S(1)}, bf16[32,512]{1,0:T(8,128)(2,1)S(1)}, u32[]{:S(2)}, u32[]{:S(2)}) collective-permute-start(bf16[32,512]{1,0:T(8,128)(2,1)S(1)} %get-tuple-element.24), channel_id=1, source_target_pairs={{0,1},{1,0},{2,3},{3,2},{4,5},{5,4},{6,7},{7,6},{8,9},{9,8},{10,11... | collective-permute-start | bytes 98312 | tf_op jit(solution)/shard_map/ppermute | solution.py:675
  5.0 4.8 %collective-permute-start.4 = (bf16[32,512]{1,0:T(8,128)(2,1)S(1)}, bf16[32,512]{1,0:T(8,128)(2,1)S(1)}, u32[]{:S(2)}, u32[]{:S(2)}) collective-permute-start(bf16[32,512]{1,0:T(8,128)(2,1)S(1)} %select_select_fusion), channel_id=1, source_target_pairs={{0,3},{4,7},{3,0},{7,4},{1,5},{2,6},{5,1},{6,2},{8,11},{12,15},{11... | collective-permute-start | bytes 98312 | tf_op jit(solution)/shard_map/ppermute | solution.py:675
  9.3 13.0 %collective-permute-start.3 = (bf16[528,512]{1,0:T(8,128)(2,1)S(1)}, bf16[528,512]{1,0:T(8,128)(2,1)S(1)}, u32[]{:S(2)}, u32[]{:S(2)}) collective-permute-start(bf16[528,512]{1,0:T(8,128)(2,1)S(1)} %first.1), channel_id=1, source_target_pairs={{0,4},{3,7},{4,0},{7,3},{1,2},{5,6},{2,1},{6,5},{8,12},{11,15},{12... | collective-permute-start | bytes 1622024 | tf_op jit(solution)/shard_map/ppermute | solution.py:675
  18.5 14.6 %collective-permute-start.5 = (bf16[528,512]{1,0:T(8,128)(2,1)S(1)}, bf16[528,512]{1,0:T(8,128)(2,1)S(1)}, u32[]{:S(2)}, u32[]{:S(2)}) collective-permute-start(bf16[528,512]{1,0:T(8,128)(2,1)S(1)} %second.1.local_ref), channel_id=1, source_target_pairs={{0,2},{3,1},{4,6},{7,5},{8,10},{11,9},{12,14},{15,13},{16,18},{19,... | collective-permute-start | bytes 1622024 | tf_op jit(solution)/shard_map/ppermute | solution.py:675
  22.9 10.2 %collective-permute-start.6 = (bf16[256,256]{1,0:T(8,128)(2,1)S(1)}, bf16[256,256]{1,0:T(8,128)(2,1)S(1)}, u32[]{:S(2)}, u32[]{:S(2)}) collective-permute-start(bf16[256,256]{1,0:T(8,128)(2,1)S(1)} %get-tuple-element.34), channel_id=1, source_target_pairs={{1,5},{2,6},{5,1},{6,2},{9,13},{10,14},{13,9},{14,10},{17,21},{18,... | collective-permute-start | bytes 393224 | tf_op jit(solution)/shard_map/ppermute | solution.py:675
  24.8 18.2 %collective-permute-start.8 = (bf16[512,512]{1,0:T(8,128)(2,1)S(1)}, bf16[512,512]{1,0:T(8,128)(2,1)S(1)}, u32[]{:S(2)}, u32[]{:S(2)}) collective-permute-start(bf16[512,512]{1,0:T(8,128)(2,1)S(1)} %get-tuple-element.37), channel_id=1, source_target_pairs={{1,5},{2,6},{5,1},{6,2},{9,13},{10,14},{13,9},{14,10},{17,21},{18,... | collective-permute-start | bytes 1572872 | tf_op jit(solution)/shard_map/ppermute | solution.py:675
  33.7 6.9 %collective-permute-start.7 = (bf16[256,256]{1,0:T(8,128)(2,1)S(1)}, bf16[256,256]{1,0:T(8,128)(2,1)S(1)}, u32[]{:S(2)}, u32[]{:S(2)}) collective-permute-start(bf16[256,256]{1,0:T(8,128)(2,1)S(1)} %get-tuple-element.36.pooled_ref), channel_id=1, source_target_pairs={{8,0},{16,8},{24,16},{9,1},{17,9},{25,17},{10,2},{18,10},{26,18},{... | collective-permute-start | bytes 393224 | tf_op jit(solution)/shard_map/ppermute | solution.py:739
  37.1 7.8 %collective-permute-start.9 = (bf16[256,256]{1,0:T(8,128)(2,1)S(1)}, bf16[256,256]{1,0:T(8,128)(2,1)S(1)}, u32[]{:S(2)}, u32[]{:S(2)}) collective-permute-start(bf16[256,256]{1,0:T(8,128)(2,1)S(1)} %get-tuple-element.36.pooled_ref), channel_id=1, source_target_pairs={{0,8},{8,16},{16,24},{1,9},{9,17},{17,25},{2,10},{10,18},{18,26},{... | collective-permute-start | bytes 393224 | tf_op jit(solution)/shard_map/ppermute | solution.py:738
